TPU v7x, 256 devices: a whole 4x4x8 slice. The times are simulated.
256 devices in a mesh: ctx: 16 (over x, y_hi, core), tp: 16 (over y_lo, z).
Axes of the slice: x: 4, y: 4 (y_hi: 2, y_lo: 2; y = y_hi * 2 + y_lo), z: 8, core: 2. Of those that a mesh axis runs over, the one named last changes fastest.
Arguments:
- out_grad: bfloat16 [4096, 8192], P('ctx', 'tp'), may hold values from -6 to 6
- query_rows: bfloat16 [4096, 8192], P('ctx', 'tp'), may hold values from -6 to 6
- key_rows: bfloat16 [4096, 8192], P('ctx', 'tp'), may hold values from -6 to 6
- value_rows: bfloat16 [4096, 8192], P('ctx', 'tp'), may hold values from -6 to 6
- conv_rows: bfloat16 [4096, 8192], P('ctx', 'tp'), may hold values from -6 to 6
- long_filter: float32 [768, 8192], P('ctx', 'tp'), may hold values from -0.21650635 to 0.21650635
- block_table: int32 [32], replicated, may hold values from 0 to 31, each once
Outputs:
- q_grad: bfloat16 [4096, 8192], P('ctx', 'tp')
- k_grad: bfloat16 [4096, 8192], P('ctx', 'tp')
- v_grad: bfloat16 [4096, 8192], P('ctx', 'tp')
- filter_grad: float32 [768, 8192], P('ctx', 'tp')
Inputs may be any that keep to these rules, and one draw needn't show every extreme that they name: slot s, block s % 2 of the device with index s // 2 along ctx, holds sequence block block_table[s]; every block appears once.
All inputs are finite; a program needn't handle non-finite values.
Results may differ from a plain program's by a relative error of at most 0.009.
Values may be sent and summed in bfloat16 or wider, within the bound.
A program may use at most 128 MiB of HBM per device.

v0:
```python
import math

import jax
import jax.numpy as jnp
from jax import lax
from jax.sharding import PartitionSpec as P

BLOCK = 128
LAG_BLOCKS = 6


HIGHEST_PRECISION = lax.Precision.HIGHEST


def dft_tables(length):
    indices = lax.iota(jnp.int32, length)
    phases = indices[:, None] * indices[None, :] % length
    angles = phases.astype(jnp.float32) * (2.0 * math.pi / length)
    return (jnp.cos(angles), jnp.sin(angles))


def forward_exact(blocks, cos_table, sine_table):
    in_rows = blocks.shape[1]
    real_part = jnp.einsum("wt,ntc->nwc", cos_table, blocks, precision=HIGHEST_PRECISION)
    imag_part = -jnp.einsum("wt,ntc->nwc", sine_table, blocks, precision=HIGHEST_PRECISION)
    return (real_part, imag_part)


def forward_low(blocks, cos_low, sine_low):
    in_rows = blocks.shape[1]
    real_part = jnp.einsum(
        "wt,ntc->nwc", cos_low[:, :in_rows], blocks, preferred_element_type=jnp.float32
    )
    imag_part = -jnp.einsum(
        "wt,ntc->nwc", sine_low[:, :in_rows], blocks, preferred_element_type=jnp.float32
    )
    return (real_part, imag_part)


def inverse(real_part, imag_part, cos_table, sine_table, out_rows):
    factor = 1.0 / cos_table.shape[0]
    cosine_part = jnp.einsum(
        "tw,nwc->ntc", cos_table[:out_rows], real_part, precision=HIGHEST_PRECISION
    )
    sine_part = jnp.einsum(
        "tw,nwc->ntc", sine_table[:out_rows], imag_part, precision=HIGHEST_PRECISION
    )
    return (cosine_part - sine_part) * factor


def filter_segments(full_filter, cos_table, sine_table):
    channels = full_filter.shape[1]
    filter_blocks = full_filter.reshape(LAG_BLOCKS, BLOCK, channels)
    zero_block = jnp.zeros((1, BLOCK, channels), jnp.float32)
    upper_half = jnp.concatenate([filter_blocks, zero_block], 0)
    lower_half = jnp.concatenate([zero_block, filter_blocks], 0)
    cyclic = jnp.concatenate([upper_half, lower_half], 1)
    return forward_exact(cyclic, cos_table, sine_table)


def settle_lags(lag_real, lag_imag, cos_table, sine_table, factor):
    times = inverse(lag_real, lag_imag, cos_table, sine_table, 2 * BLOCK)
    lagged = (times[:-1, :BLOCK] + times[1:, BLOCK:]) * factor
    return lagged.reshape(-1, times.shape[2])


def empty_state(slots, channels):
    slot_zeros = jnp.zeros((slots, 2 * BLOCK, channels), jnp.float32)
    lag_zeros = jnp.zeros((LAG_BLOCKS + 1, 2 * BLOCK, channels), jnp.float32)
    return (slot_zeros, slot_zeros, lag_zeros, lag_zeros)


def make_absorb(block_table, local_ids, spectra, cos_low, sine_low):
    prod_real, prod_imag, seg_real, seg_imag = spectra
    last_seg = LAG_BLOCKS

    def absorb(carried, incoming, first_slot):

        def absorb_block(state, member):
            grad_block, offset = member
            lag_index = block_table[offset] - local_ids
            inside_flag = (lag_index >= 0) & (lag_index <= last_seg)

            def update(current):
                grad_real, grad_imag = forward_low(grad_block[None], cos_low, sine_low)
                inside = inside_flag.astype(jnp.float32)[:, None, None]
                chosen = jnp.clip(lag_index, 0, last_seg)
                pick_real = seg_real[chosen]
                pick_imag = seg_imag[chosen]
                du_real, du_imag, lag_real, lag_imag = current
                du_real = du_real + inside * (pick_real * grad_real + pick_imag * grad_imag)
                du_imag = du_imag + inside * (pick_real * grad_imag - pick_imag * grad_real)
                lag_real = lag_real.at[chosen].add(
                    inside * (prod_real * grad_real + prod_imag * grad_imag)
                )
                lag_imag = lag_imag.at[chosen].add(
                    inside * (prod_real * grad_imag - prod_imag * grad_real)
                )
                return (du_real, du_imag, lag_real, lag_imag)

            def unchanged(current):
                return current

            state = lax.cond(jnp.any(inside_flag), update, unchanged, state)
            return (state, None)

        offsets = lax.iota(jnp.int32, incoming.shape[0])
        carried, unused = lax.scan(absorb_block, carried, (incoming, offsets))
        return carried

    return absorb


def on_device(out_grad, query_rows, key_rows, value_rows, conv_rows, long_filter, block_table):
    ranks = lax.axis_size("ctx")
    device = lax.axis_index("ctx")
    channels = out_grad.shape[1]
    factor = (2.0 * BLOCK * ranks) ** (-0.5)
    cos_table, sine_table = dft_tables(2 * BLOCK)
    cos_low = cos_table.astype(jnp.bfloat16)
    sine_low = sine_table.astype(jnp.bfloat16)
    grad_f = out_grad.astype(jnp.float32)
    key_f = key_rows.astype(jnp.float32)
    value_f = value_rows.astype(jnp.float32)
    q_grad = (grad_f * conv_rows.astype(jnp.float32)).astype(jnp.bfloat16)
    weighted = (grad_f * query_rows.astype(jnp.float32)).astype(jnp.bfloat16)
    product = (key_f * value_f).astype(jnp.bfloat16)
    full_filter = lax.all_gather(long_filter, "ctx", axis=0, tiled=True)
    local_ids = lax.dynamic_slice_in_dim(block_table, 2 * device, 2)
    seg_real, seg_imag = filter_segments(full_filter, cos_table, sine_table)
    prod_real, prod_imag = forward_low(product.reshape(2, BLOCK, channels), cos_low, sine_low)
    absorb = make_absorb(
        block_table, local_ids, (prod_real, prod_imag, seg_real, seg_imag), cos_low, sine_low
    )
    carried = absorb(
        empty_state(2, channels),
        lax.all_gather(weighted.reshape(2, BLOCK, channels), "ctx", axis=0, tiled=True),
        jnp.int32(0),
    )
    du_real, du_imag, lag_real, lag_imag = carried
    seq_grad = inverse(du_real, du_imag, cos_table, sine_table, BLOCK).reshape(2 * BLOCK, channels)
    lag_rows = settle_lags(lag_real, lag_imag, cos_table, sine_table, factor)
    own_rows = LAG_BLOCKS * BLOCK // ranks
    summed = lax.psum(lag_rows, "ctx")
    filter_raw = lax.dynamic_slice_in_dim(summed, device * own_rows, own_rows, 0)
    k_grad = (seq_grad * value_f).astype(jnp.bfloat16)
    v_grad = (seq_grad * key_f).astype(jnp.bfloat16)
    return (q_grad, k_grad, v_grad, filter_raw)


def solution(mesh):
    in_specs = (
        P("ctx", "tp"),
        P("ctx", "tp"),
        P("ctx", "tp"),
        P("ctx", "tp"),
        P("ctx", "tp"),
        P("ctx", "tp"),
        P(),
    )
    out_specs = (P("ctx", "tp"), P("ctx", "tp"), P("ctx", "tp"), P("ctx", "tp"))
    return jax.shard_map(
        on_device, mesh=mesh, in_specs=in_specs, out_specs=out_specs, check_vma=False
    )
```

profile of v0, /device:TPU:1, one launch (start us, length us, event | category | flops | bytes accessed | tf_op | source)
XLA Modules:
  0.0 815.4 jit_solution(8108745224471367392)
XLA Ops:
  17.3 49.4 %all-gather.3.cloned.1.call-done = f32[768,512]{1,0:T(8,128)} async-done(((f32[48,512]{1,0:T(8,128)}), f32[768,512]{1,0:T(8,128)}) %all-gather.3.cloned.1.call-update) | async-done | bytes 1572880 | tf_op jit(solution)/shard_map/all_gather | solution.py:128
  68.6 5.9 fusion.22
  79.1 5.9 negate_bitcast_fusion
  89.6 40.5 %all-gather.5.cloned.1.call-done = bf16[32,128,512]{2,1,0:T(8,128)(2,1)} async-done(((bf16[2,128,512]{2,1,0:T(8,128)(2,1)}), bf16[32,128,512]{2,1,0:T(8,128)(2,1)}) %all-gather.5.cloned.1.call-update) | async-done | bytes 4194320 | tf_op jit(solution)/shard_map/all_gather | solution.py:137
  135.0 512.9 %while.17 = (s32[]{:T(128)}, f32[2,256,512]{2,1,0:T(8,128)S(1)}, f32[2,256,512]{2,1,0:T(8,128)S(1)}, f32[7,256,512]{2,1,0:T(8,128)}, f32[7,256,512]{2,1,0:T(8,12...) while((s32[]{:T(128)}, f32[2,256,512]{2,1,0:T(8,128)S(1)}, ...), condition=%wide.region_6.7_spmd.clone, body=%wide.region_0.6_spmd.clone.sunk | while | flops 73532448 | bytes 42604128 | solution.py:108
  147.3 22.2 %conditional.3 = ((f32[2,256,512]{2,1,0:T(8,128)S(1)}, f32[2,256,512]{2,1,0:T(8,128)S(1)}, f32[7,256,512]{2,1,0:T(8,128)}, f32[7,256,512]{2,1,0:T(8,128)})) conditional(s32[]{:T(128)} %convert_element_type.164, (f32[2,256,512]{2,1,0:T(8,128)S(1)}, f32[2,256,512]{2,1,0:T(8,128)S(1)}, f32[7,256,512]{2,1,0:T(8,128)}, ...), branch_computations={%region_2.2_spmd, %region_3.5_spmd} | conditional | flops 72483848 | bytes 42341600 | solution.py:104
  158.1 5.2 subtract_multiply_fusion
  175.7 22.2 %conditional.3 = ((f32[2,256,512]{2,1,0:T(8,128)S(1)}, f32[2,256,512]{2,1,0:T(8,128)S(1)}, f32[7,256,512]{2,1,0:T(8,128)}, f32[7,256,512]{2,1,0:T(8,128)})) conditional(s32[]{:T(128)} %convert_element_type.164, (f32[2,256,512]{2,1,0:T(8,128)S(1)}, f32[2,256,512]{2,1,0:T(8,128)S(1)}, f32[7,256,512]{2,1,0:T(8,128)}, ...), branch_computations={%region_2.2_spmd, %region_3.5_spmd} | conditional | flops 72483848 | bytes 42341600 | solution.py:104
  186.4 5.2 subtract_multiply_fusion
  204.0 22.5 %conditional.3 = ((f32[2,256,512]{2,1,0:T(8,128)S(1)}, f32[2,256,512]{2,1,0:T(8,128)S(1)}, f32[7,256,512]{2,1,0:T(8,128)}, f32[7,256,512]{2,1,0:T(8,128)})) conditional(s32[]{:T(128)} %convert_element_type.164, (f32[2,256,512]{2,1,0:T(8,128)S(1)}, f32[2,256,512]{2,1,0:T(8,128)S(1)}, f32[7,256,512]{2,1,0:T(8,128)}, ...), branch_computations={%region_2.2_spmd, %region_3.5_spmd} | conditional | flops 72483848 | bytes 42341600 | solution.py:104
  214.8 5.2 subtract_multiply_fusion
  232.7 22.5 %conditional.3 = ((f32[2,256,512]{2,1,0:T(8,128)S(1)}, f32[2,256,512]{2,1,0:T(8,128)S(1)}, f32[7,256,512]{2,1,0:T(8,128)}, f32[7,256,512]{2,1,0:T(8,128)})) conditional(s32[]{:T(128)} %convert_element_type.164, (f32[2,256,512]{2,1,0:T(8,128)S(1)}, f32[2,256,512]{2,1,0:T(8,128)S(1)}, f32[7,256,512]{2,1,0:T(8,128)}, ...), branch_computations={%region_2.2_spmd, %region_3.5_spmd} | conditional | flops 72483848 | bytes 42341600 | solution.py:104
  243.4 5.2 subtract_multiply_fusion
  273.8 22.5 %conditional.3 = ((f32[2,256,512]{2,1,0:T(8,128)S(1)}, f32[2,256,512]{2,1,0:T(8,128)S(1)}, f32[7,256,512]{2,1,0:T(8,128)}, f32[7,256,512]{2,1,0:T(8,128)})) conditional(s32[]{:T(128)} %convert_element_type.164, (f32[2,256,512]{2,1,0:T(8,128)S(1)}, f32[2,256,512]{2,1,0:T(8,128)S(1)}, f32[7,256,512]{2,1,0:T(8,128)}, ...), branch_computations={%region_2.2_spmd, %region_3.5_spmd} | conditional | flops 72483848 | bytes 42341600 | solution.py:104
  284.5 5.2 subtract_multiply_fusion
  321.1 22.5 %conditional.3 = ((f32[2,256,512]{2,1,0:T(8,128)S(1)}, f32[2,256,512]{2,1,0:T(8,128)S(1)}, f32[7,256,512]{2,1,0:T(8,128)}, f32[7,256,512]{2,1,0:T(8,128)})) conditional(s32[]{:T(128)} %convert_element_type.164, (f32[2,256,512]{2,1,0:T(8,128)S(1)}, f32[2,256,512]{2,1,0:T(8,128)S(1)}, f32[7,256,512]{2,1,0:T(8,128)}, ...), branch_computations={%region_2.2_spmd, %region_3.5_spmd} | conditional | flops 72483848 | bytes 42341600 | solution.py:104
  331.8 5.2 subtract_multiply_fusion
  380.8 22.6 %conditional.3 = ((f32[2,256,512]{2,1,0:T(8,128)S(1)}, f32[2,256,512]{2,1,0:T(8,128)S(1)}, f32[7,256,512]{2,1,0:T(8,128)}, f32[7,256,512]{2,1,0:T(8,128)})) conditional(s32[]{:T(128)} %convert_element_type.164, (f32[2,256,512]{2,1,0:T(8,128)S(1)}, f32[2,256,512]{2,1,0:T(8,128)S(1)}, f32[7,256,512]{2,1,0:T(8,128)}, ...), branch_computations={%region_2.2_spmd, %region_3.5_spmd} | conditional | flops 72483848 | bytes 42341600 | solution.py:104
  391.6 5.2 subtract_multiply_fusion
  415.8 22.5 %conditional.3 = ((f32[2,256,512]{2,1,0:T(8,128)S(1)}, f32[2,256,512]{2,1,0:T(8,128)S(1)}, f32[7,256,512]{2,1,0:T(8,128)}, f32[7,256,512]{2,1,0:T(8,128)})) conditional(s32[]{:T(128)} %convert_element_type.164, (f32[2,256,512]{2,1,0:T(8,128)S(1)}, f32[2,256,512]{2,1,0:T(8,128)S(1)}, f32[7,256,512]{2,1,0:T(8,128)}, ...), branch_computations={%region_2.2_spmd, %region_3.5_spmd} | conditional | flops 72483848 | bytes 42341600 | solution.py:104
  426.6 5.2 subtract_multiply_fusion
  450.7 22.5 %conditional.3 = ((f32[2,256,512]{2,1,0:T(8,128)S(1)}, f32[2,256,512]{2,1,0:T(8,128)S(1)}, f32[7,256,512]{2,1,0:T(8,128)}, f32[7,256,512]{2,1,0:T(8,128)})) conditional(s32[]{:T(128)} %convert_element_type.164, (f32[2,256,512]{2,1,0:T(8,128)S(1)}, f32[2,256,512]{2,1,0:T(8,128)S(1)}, f32[7,256,512]{2,1,0:T(8,128)}, ...), branch_computations={%region_2.2_spmd, %region_3.5_spmd} | conditional | flops 72483848 | bytes 42341600 | solution.py:104
  479.4 22.5 %conditional.3 = ((f32[2,256,512]{2,1,0:T(8,128)S(1)}, f32[2,256,512]{2,1,0:T(8,128)S(1)}, f32[7,256,512]{2,1,0:T(8,128)}, f32[7,256,512]{2,1,0:T(8,128)})) conditional(s32[]{:T(128)} %convert_element_type.164, (f32[2,256,512]{2,1,0:T(8,128)S(1)}, f32[2,256,512]{2,1,0:T(8,128)S(1)}, f32[7,256,512]{2,1,0:T(8,128)}, ...), branch_computations={%region_2.2_spmd, %region_3.5_spmd} | conditional | flops 72483848 | bytes 42341600 | solution.py:104
  490.2 5.2 subtract_multiply_fusion
  514.3 22.6 %conditional.3 = ((f32[2,256,512]{2,1,0:T(8,128)S(1)}, f32[2,256,512]{2,1,0:T(8,128)S(1)}, f32[7,256,512]{2,1,0:T(8,128)}, f32[7,256,512]{2,1,0:T(8,128)})) conditional(s32[]{:T(128)} %convert_element_type.164, (f32[2,256,512]{2,1,0:T(8,128)S(1)}, f32[2,256,512]{2,1,0:T(8,128)S(1)}, f32[7,256,512]{2,1,0:T(8,128)}, ...), branch_computations={%region_2.2_spmd, %region_3.5_spmd} | conditional | flops 72483848 | bytes 42341600 | solution.py:104
  549.3 22.5 %conditional.3 = ((f32[2,256,512]{2,1,0:T(8,128)S(1)}, f32[2,256,512]{2,1,0:T(8,128)S(1)}, f32[7,256,512]{2,1,0:T(8,128)}, f32[7,256,512]{2,1,0:T(8,128)})) conditional(s32[]{:T(128)} %convert_element_type.164, (f32[2,256,512]{2,1,0:T(8,128)S(1)}, f32[2,256,512]{2,1,0:T(8,128)S(1)}, f32[7,256,512]{2,1,0:T(8,128)}, ...), branch_computations={%region_2.2_spmd, %region_3.5_spmd} | conditional | flops 72483848 | bytes 42341600 | solution.py:104
  578.0 22.5 %conditional.3 = ((f32[2,256,512]{2,1,0:T(8,128)S(1)}, f32[2,256,512]{2,1,0:T(8,128)S(1)}, f32[7,256,512]{2,1,0:T(8,128)}, f32[7,256,512]{2,1,0:T(8,128)})) conditional(s32[]{:T(128)} %convert_element_type.164, (f32[2,256,512]{2,1,0:T(8,128)S(1)}, f32[2,256,512]{2,1,0:T(8,128)S(1)}, f32[7,256,512]{2,1,0:T(8,128)}, ...), branch_computations={%region_2.2_spmd, %region_3.5_spmd} | conditional | flops 72483848 | bytes 42341600 | solution.py:104
  588.7 5.2 subtract_multiply_fusion
  625.3 22.6 %conditional.3 = ((f32[2,256,512]{2,1,0:T(8,128)S(1)}, f32[2,256,512]{2,1,0:T(8,128)S(1)}, f32[7,256,512]{2,1,0:T(8,128)}, f32[7,256,512]{2,1,0:T(8,128)})) conditional(s32[]{:T(128)} %convert_element_type.164, (f32[2,256,512]{2,1,0:T(8,128)S(1)}, f32[2,256,512]{2,1,0:T(8,128)S(1)}, f32[7,256,512]{2,1,0:T(8,128)}, ...), branch_computations={%region_2.2_spmd, %region_3.5_spmd} | conditional | flops 72483848 | bytes 42341600 | solution.py:104
  647.8 7.1 fusion.40
  654.9 5.3 multiply_bitcast_fusion
  664.2 143.2 %all-reduce.4.cloned.1.call-done = f32[768,512]{1,0:T(8,128)} async-done(((f32[768,512]{1,0:T(8,128)}), f32[768,512]{1,0:T(8,128)}) %all-reduce.4.cloned.1.call-update) | async-done | bytes 1572880 | tf_op jit(solution)/shard_map/psum | solution.py:144
  (492 shorter events, 406.6 us)
Async XLA Ops:
  7.2 59.6 %all-gather.3.cloned.1.call-start = ((), (), s32[]{:S(2)}) async-start(), calls=%async_computation | async-start | bytes 1671168 | tf_op jit(solution)/shard_map/all_gather | solution.py:128
  7.9 122.2 %all-gather.5.cloned.1.call-start = ((), (), s32[]{:S(2)}) async-start(), calls=%async_computation.1 | async-start | bytes 4456448 | tf_op jit(solution)/shard_map/all_gather | solution.py:137
  10.0 797.4 %all-reduce.4.cloned.1.call-start = ((), (), s32[]{:S(2)}) async-start(), calls=%async_computation.2 | async-start | bytes 3145728 | tf_op jit(solution)/shard_map/psum | solution.py:144
  163.3 6.2 copy-start.1
  163.3 6.2 copy-start.3
  191.6 6.2 copy-start.1
  191.6 6.2 copy-start.3
  220.0 6.5 copy-start.1
  220.0 6.5 copy-start.3
  248.7 6.5 copy-start.1
  248.7 6.5 copy-start.3
  289.8 6.5 copy-start.1
  289.8 6.5 copy-start.3
  337.1 6.6 copy-start.1
  337.1 6.6 copy-start.3
  396.8 6.6 copy-start.1
  396.8 6.6 copy-start.3
  431.8 6.6 copy-start.1
  431.8 6.6 copy-start.3
  466.7 6.6 copy-start.1
  466.7 6.6 copy-start.3
  495.4 6.6 copy-start.1
  495.4 6.6 copy-start.3
  530.3 6.6 copy-start.1
  530.3 6.6 copy-start.3
  565.3 6.5 copy-start.1
  565.3 6.5 copy-start.3
  593.9 6.5 copy-start.1
  593.9 6.5 copy-start.3
  641.3 6.6 copy-start.1
  641.3 6.6 copy-start.3
  647.8 7.1 copy-start.4
  (35 other events, 80.4 us)
Sparse Core Ops, SparseCore 0:
  10.7 56.0 all-gather.2
  70.0 60.0 all-gather.4
  661.9 145.4 all-reduce.3
where the time goes:
time: 819 us; the launch traced here: 815 us
  other arithmetic  248 us (30%)
  waiting for transfers between devices  234 us (29%)
  local copies, waits for them, and re-layouts  175 us (21%)
  loops' own time  85.6 us (10%)
  matrix products  58.4 us (7%)
  between operations  13.9 us (2%)
    psum x1, waiting for transfers between devices, on_device(): summed = lax.psum(lag_rows, 'ctx')  143 us
    another operation x1, loops' own time, absorb(): carried, unused = lax.scan(absorb_block, carried, (incoming, offsets))  84 us
    mul x14, other arithmetic, update(): inside * (prod_real * grad_imag - prod_imag * grad_real)  73.2 us
    all_gather x1, waiting for transfers between devices, on_device(): full_filter = lax.all_gather(long_filter, 'ctx', axis=0, tiled=True)  49.4 us
    scatter-add x14, other arithmetic, update(): lag_imag.at[chosen]  48.5 us
    scatter-add x14, other arithmetic, update(): lag_real.at[chosen]  42.6 us
    all_gather x1, waiting for transfers between devices, on_device(): lax.all_gather(weighted.reshape(2, BLOCK, channels), 'ctx', axis=0, tiled...  40.5 us
    gather x14, local copies, waits for them, and re-layouts, update(): pick_imag = seg_imag[chosen]  37.1 us
  transfers between devices with their start and end apart: 3, of which 3 were waited for; matrix products, arithmetic and copies ran while one was open for 4% of the time, Pallas kernels for 0%

commit v1 on v0

v1 whole, which is shorter than its diff:
```python
import functools

import jax
import jax.numpy as jnp
import numpy as np
from jax import lax
from jax.experimental import pallas as pl
from jax.experimental.pallas import tpu as pltpu
from jax.sharding import PartitionSpec as P

BLOCK = 128
LAG_BLOCKS = 6
SPAN = 2 * BLOCK
RANKS = 16
SLOTS = 2 * RANKS
MESH = pl.DeviceIdType.MESH
F32 = jnp.float32
BF16 = jnp.bfloat16
NT = (((1,), (1,)), ((), ()))


def tables():
    time = np.arange(SPAN)[:, None]
    bins = np.arange(BLOCK)[None, :] + 0.5
    angles = 2.0 * np.pi * time * bins / SPAN
    forward = np.concatenate([np.cos(angles), -np.sin(angles)], 1)
    back = np.concatenate([np.cos(angles[:BLOCK]).T, -np.sin(angles[:BLOCK]).T], 0) * (2.0 / SPAN)
    return jnp.asarray(forward, BF16), jnp.asarray(back, BF16), jnp.asarray(np.eye(SPAN), BF16)


def dot(left, right):
    return jnp.dot(left, right, preferred_element_type=F32)


def flip(eye, rows):
    return lax.dot_general(eye, rows, NT, preferred_element_type=F32)


def peer(me, offset):
    dx, dy, dc = offset
    x = lax.rem(lax.div(me, 4) + dx, 4)
    y = lax.rem(lax.rem(lax.div(me, 2), 2) + dy, 2)
    c = lax.rem(lax.rem(me, 2) + dc, 2)
    return (x * 2 + y) * 2 + c


OFFSETS = sorted(
    [(dx, dy, dc) for dx in range(4) for dy in range(2) for dc in range(2)][1:],
    key=lambda o: -(min(o[0], 4 - o[0]) + 2 * o[1] + o[2]),
)


def exchange_kernel(
    table, grad, query, key, value, taps, forward, back, eye, out,
    inverse, send_a, recv_a, send_b, spec_v, spec_u, spec_h, spec_d, spec_f,
    a_send, a_recv, b_send, b_recv, own_sem,
):
    me = lax.axis_index("ctx")
    barrier = pltpu.get_barrier_semaphore()
    for offset in OFFSETS:
        pl.semaphore_signal(barrier, inc=1, device_id={"ctx": peer(me, offset)}, device_id_type=MESH)

    unit = eye[...]
    for which, (left, right) in enumerate(((grad, query), (key, value))):
        product = (left[...].astype(F32) * right[...].astype(F32)).astype(BF16)
        for half in range(2):
            turned = flip(unit, product[:, half * SPAN:(half + 1) * SPAN]).astype(BF16)
            for piece in range(8):
                rows = turned[piece * 32:(piece + 1) * 32]
                send_a[half * 8 + piece, 2 * which] = rows[:, :BLOCK]
                send_a[half * 8 + piece, 2 * which + 1] = rows[:, BLOCK:]
    lags = taps.shape[0]
    padded = jnp.concatenate([taps[...].astype(BF16), jnp.zeros((BLOCK - lags, taps.shape[1]), BF16)], 0)
    for half in range(2):
        turned = flip(unit, padded[:, half * SPAN:(half + 1) * SPAN]).astype(BF16)
        for piece in range(8):
            send_a[half * 8 + piece, 4] = turned[piece * 32:(piece + 1) * 32]

    pl.semaphore_wait(barrier, len(OFFSETS))
    copies = []
    for i, offset in enumerate(OFFSETS):
        to = peer(me, offset)
        copy = pltpu.make_async_remote_copy(
            send_a.at[to], recv_a.at[me], a_send.at[i], a_recv.at[i],
            device_id={"ctx": to}, device_id_type=MESH,
        )
        copy.start()
        copies.append(copy)
    own = pltpu.make_async_copy(send_a.at[me], recv_a.at[me], own_sem)
    own.start()

    def slot_of(p, carry):
        found = jnp.int32(0)
        for s in range(SLOTS):
            found = jnp.where(table[s] == p, s, found)
        inverse[p] = found
        return carry

    lax.fori_loop(0, SLOTS, slot_of, 0)
    own.wait()
    for copy in copies:
        copy.wait()

    lane = lax.broadcasted_iota(jnp.int32, (32, BLOCK), 1)
    order = [jnp.zeros((32, BLOCK), F32) for _ in range(LAG_BLOCKS)]
    for src in range(RANKS):
        first, shift = divmod(src * lags, BLOCK)
        rows = recv_a[src, 4].astype(F32)
        if shift:
            rows = pltpu.roll(rows, shift, 1)
        if shift + lags > BLOCK:
            order[first] = order[first] + jnp.where(lane >= shift, rows, 0.0)
            order[first + 1] = order[first + 1] + jnp.where(lane < shift, rows, 0.0)
        else:
            order[first] = order[first] + rows
    half_forward = forward[:BLOCK]
    spec_h[...] = dot(jnp.concatenate(order, 0).astype(BF16), half_forward).reshape(LAG_BLOCKS, 32, SPAN)

    full_forward = forward[...]
    chunk = 8
    for start in range(0, SLOTS, chunk):
        rows_w = []
        rows_u = []
        for p in range(start, start + chunk + 1):
            if p < SLOTS:
                slot = inverse[p]
                src = lax.div(slot, 2)
                b = lax.rem(slot, 2)
                rows_w.append(recv_a[src, b])
                if p < start + chunk:
                    rows_u.append(recv_a[src, 2 + b])
            else:
                rows_w.append(jnp.zeros((32, BLOCK), BF16))
        window = jnp.concatenate(
            [jnp.concatenate(rows_w[:-1], 0), jnp.concatenate(rows_w[1:], 0)], 1
        )
        spec_v[start:start + chunk] = dot(window, full_forward).reshape(chunk, 32, SPAN)
        spec_u[start:start + chunk] = dot(jnp.concatenate(rows_u, 0), half_forward).reshape(chunk, 32, SPAN)

    def group(g, carry):
        rows = pl.ds(pl.multiple_of(g * 8, 8), 8)
        h_re = [spec_h[m, rows, :BLOCK] for m in range(LAG_BLOCKS)]
        h_im = [spec_h[m, rows, BLOCK:] for m in range(LAG_BLOCKS)]
        f_re = [jnp.zeros((8, BLOCK), F32) for _ in range(LAG_BLOCKS)]
        f_im = [jnp.zeros((8, BLOCK), F32) for _ in range(LAG_BLOCKS)]
        for p in range(SLOTS):
            u_re, u_im = spec_u[p, rows, :BLOCK], spec_u[p, rows, BLOCK:]
            d_re = d_im = None
            for m in range(min(LAG_BLOCKS, SLOTS - p)):
                v_re, v_im = spec_v[p + m, rows, :BLOCK], spec_v[p + m, rows, BLOCK:]
                f_re[m] += u_re * v_re + u_im * v_im
                f_im[m] += u_re * v_im - u_im * v_re
                t_re = h_re[m] * v_re + h_im[m] * v_im
                t_im = h_re[m] * v_im - h_im[m] * v_re
                d_re = t_re if d_re is None else d_re + t_re
                d_im = t_im if d_im is None else d_im + t_im
            spec_d[p, rows, :BLOCK] = d_re
            spec_d[p, rows, BLOCK:] = d_im
        for m in range(LAG_BLOCKS):
            spec_f[m, rows, :BLOCK] = f_re[m]
            spec_f[m, rows, BLOCK:] = f_im[m]
        return carry

    lax.fori_loop(0, 4, group, 0)

    inverted = back[...]
    for start in range(0, SLOTS, chunk):
        rows_d = [spec_d[table[s]].astype(BF16) for s in range(start, start + chunk)]
        result = dot(jnp.concatenate(rows_d, 0), inverted).astype(BF16)
        for i in range(chunk):
            send_b[(start + i) // 2, (start + i) % 2] = result[i * 32:(i + 1) * 32]
    scale = float((SLOTS * BLOCK) ** -0.5)
    lagged = dot(spec_f[...].reshape(LAG_BLOCKS * 32, SPAN).astype(BF16), inverted) * scale
    for to in range(RANKS):
        first, shift = divmod(to * lags, BLOCK)
        rows = lagged[first * 32:(first + 1) * 32]
        if shift:
            rows = pltpu.roll(rows, BLOCK - shift, 1)
        if shift + lags > BLOCK:
            later = pltpu.roll(lagged[(first + 1) * 32:(first + 2) * 32], BLOCK - shift, 1)
            rows = jnp.where(lane < BLOCK - shift, rows, later)
        send_b[to, 2] = rows.astype(BF16)

    copies = []
    for i, offset in enumerate(OFFSETS):
        to = peer(me, offset)
        copy = pltpu.make_async_remote_copy(
            send_b.at[to], out.at[me], b_send.at[i], b_recv.at[i],
            device_id={"ctx": to}, device_id_type=MESH,
        )
        copy.start()
        copies.append(copy)
    own = pltpu.make_async_copy(send_b.at[me], out.at[me], own_sem)
    own.start()
    own.wait()
    for copy in copies:
        copy.wait()


def finish_kernel(grad, conv, key, value, eye, pieces, q_out, k_out, v_out, f_out):
    q_out[...] = (grad[...].astype(F32) * conv[...].astype(F32)).astype(BF16)
    unit = eye[:BLOCK, :BLOCK]
    channels = grad.shape[1]
    for b in range(2):
        rows = slice(b * BLOCK, (b + 1) * BLOCK)
        turned = flip(unit, pieces[:, b].reshape(channels, BLOCK))
        k_out[rows] = (turned * value[rows].astype(F32)).astype(BF16)
        v_out[rows] = (turned * key[rows].astype(F32)).astype(BF16)
    f_out[...] = flip(unit[:f_out.shape[0]], pieces[:, 2].reshape(channels, BLOCK))


def on_device(out_grad, query_rows, key_rows, value_rows, conv_rows, long_filter, block_table):
    forward, back, eye = tables()
    vmem = pl.BlockSpec(memory_space=pltpu.VMEM)
    units = (RANKS, 3, 32, BLOCK)
    dma = pltpu.SemaphoreType.DMA
    pieces = pl.pallas_call(
        exchange_kernel,
        name="exchange",
        out_shape=jax.ShapeDtypeStruct(units, BF16),
        in_specs=[pl.BlockSpec(memory_space=pltpu.SMEM)] + [vmem] * 8,
        out_specs=vmem,
        scratch_shapes=[
            pltpu.SMEM((SLOTS,), jnp.int32),
            pltpu.VMEM((RANKS, 5, 32, BLOCK), BF16),
            pltpu.VMEM((RANKS, 5, 32, BLOCK), BF16),
            pltpu.VMEM(units, BF16),
            pltpu.VMEM((SLOTS, 32, SPAN), F32),
            pltpu.VMEM((SLOTS, 32, SPAN), F32),
            pltpu.VMEM((LAG_BLOCKS, 32, SPAN), F32),
            pltpu.VMEM((SLOTS, 32, SPAN), F32),
            pltpu.VMEM((LAG_BLOCKS, 32, SPAN), F32),
            dma((15,)), dma((15,)), dma((15,)), dma((15,)), dma,
        ],
        compiler_params=pltpu.CompilerParams(
            collective_id=0, has_side_effects=True, vmem_limit_bytes=40 * 1024 * 1024
        ),
    )(block_table, out_grad, query_rows, key_rows, value_rows, long_filter, forward, back, eye)
    rows = jax.ShapeDtypeStruct(out_grad.shape, BF16)
    return pl.pallas_call(
        finish_kernel,
        name="finish",
        out_shape=(rows, rows, rows, jax.ShapeDtypeStruct(long_filter.shape, F32)),
        in_specs=[vmem] * 6,
        out_specs=[vmem] * 4,
        compiler_params=pltpu.CompilerParams(vmem_limit_bytes=40 * 1024 * 1024),
    )(out_grad, conv_rows, key_rows, value_rows, eye, pieces)


def solution(mesh):
    rows = P("ctx", "tp")
    return jax.shard_map(
        on_device, mesh=mesh, in_specs=(rows,) * 6 + (P(),), out_specs=(rows,) * 4, check_vma=False
    )
```

time: 819 us -> 36.4 us (0.04)
  other arithmetic: 248 us -> 0 us
  waiting for transfers between devices: 234 us -> 0 us
  local copies, waits for them, and re-layouts: 175 us -> 8 us
  loops' own time: 85.6 us -> 0 us
  matrix products: 58.4 us -> 0 us
  Pallas kernels: 0 us -> 27.3 us
  between operations: 13.9 us -> 0.71 us
    psum x1 -> x0, waiting for transfers between devices: 143 us -> none  [on_device(): summed = lax.psum(lag_rows, 'ctx')]
    scatter-add x28 -> x0, other arithmetic: 91.1 us -> none  [the longest x14 48.5 us: update(): lag_imag.at[chosen]]
    all_gather x2 -> x0, waiting for transfers between devices: 89.9 us -> none  [the longest x1 49.4 us: on_device(): full_filter = lax.all_gather(long_filter, 'ctx', axis=0, tiled=True)]
    another operation x33 -> x0, loops' own time: 85.6 us -> none  [the longest x1 84 us: absorb(): carried, unused = lax.scan(absorb_block, carried, (incoming, offsets))]
    mul x15 -> x0, other arithmetic: 74.7 us -> none  [the longest x14 73.2 us: update(): inside * (prod_real * grad_imag - prod_imag * grad_real)]
    gather x28 -> x0, local copies, waits for them, and re-layouts: 74.2 us -> none  [the longest x14 37.1 us: update(): pick_imag = seg_imag[chosen]]
    dot_general x36 -> x0, matrix products: 58.4 us -> none  [the longest x15 16.4 us: forward_low(): jnp.einsum('wt,ntc->nwc', cos_low[:, :in_rows], blocks, preferred_element...]
    convert_element_type x49 -> x0, other arithmetic: 39.3 us -> none  [the longest x32 35.1 us: on_device(): sine_low = sine_table.astype(jnp.bfloat16)]
  transfers between devices with their start and end apart: 3 -> 0, of which waited for: 3 -> 0; matrix products, arithmetic and copies ran while one was open for 4% -> 0% of each run, Pallas kernels for 0% -> 0%
where the time goes in v1:
time: 36.4 us; the launch traced here: 36 us
  Pallas kernels  27.3 us (75%)
  local copies, waits for them, and re-layouts  8 us (22%)
  between operations  0.71 us (2%)
    pallas_call x1, Pallas kernels, on_device(): pl.pallas_call(exchange_kernel, name='exchange', out_shape=jax.ShapeDtype...  26.2 us
    unnamed x28, local copies, waits for them, and re-layouts  8 us
    pallas_call x1, Pallas kernels, on_device(): pl.pallas_call(finish_kernel, name='finish', out_shape=(rows, rows, rows,...  1.15 us

profile of v1, /device:TPU:1, one launch (start us, length us, event | category | flops | bytes accessed | tf_op | source)
XLA Modules:
  0.0 36.0 jit_solution(12213601008642470230)
XLA Ops:
  0.6 0.0 copy-start
  0.6 0.9 %copy-done = bf16[256,512]{1,0:T(8,128)(2,1)S(1)} copy-done((bf16[256,512]{1,0:T(8,128)(2,1)S(1)}, bf16[256,512]{1,0:T(8,128)(2,1)}, u32[]{:S(2)}) %copy-start) | copy-done | bytes 262168
  1.6 0.0 copy-start.2
  1.6 0.9 %copy-done.2 = bf16[256,512]{1,0:T(8,128)(2,1)S(1)} copy-done((bf16[256,512]{1,0:T(8,128)(2,1)S(1)}, bf16[256,512]{1,0:T(8,128)(2,1)}, u32[]{:S(2)}) %copy-start.2) | copy-done | bytes 262168
  2.5 0.0 copy-start.4
  2.5 0.9 %copy-done.4 = bf16[256,512]{1,0:T(8,128)(2,1)S(1)} copy-done((bf16[256,512]{1,0:T(8,128)(2,1)S(1)}, bf16[256,512]{1,0:T(8,128)(2,1)}, u32[]{:S(2)}) %copy-start.4) | copy-done | bytes 262168
  3.5 0.0 copy-start.6
  3.5 0.9 %copy-done.6 = bf16[256,256]{1,0:T(8,128)(2,1)S(1)} copy-done((bf16[256,256]{1,0:T(8,128)(2,1)S(1)}, bf16[256,256]{1,0:T(8,128)(2,1)}, u32[]{:S(2)}) %copy-start.6) | copy-done | bytes 131096
  4.4 0.0 copy-start.8
  4.4 0.9 %copy-done.8 = bf16[256,512]{1,0:T(8,128)(2,1)S(1)} copy-done((bf16[256,512]{1,0:T(8,128)(2,1)S(1)}, bf16[256,512]{1,0:T(8,128)(2,1)}, u32[]{:S(2)}) %copy-start.8) | copy-done | bytes 262168
  5.3 0.0 copy-start.10
  5.3 0.9 %copy-done.10 = bf16[256,256]{1,0:T(8,128)(2,1)S(1)} copy-done((bf16[256,256]{1,0:T(8,128)(2,1)S(1)}, bf16[256,256]{1,0:T(8,128)(2,1)}, u32[]{:S(2)}) %copy-start.10) | copy-done | bytes 131096
  6.2 0.0 copy-start.11
  6.2 0.9 %copy-done.11 = f32[48,512]{1,0:T(8,128)S(1)} copy-done((f32[48,512]{1,0:T(8,128)S(1)}, f32[48,512]{1,0:T(8,128)}, u32[]{:S(2)}) %copy-start.11) | copy-done | bytes 98328
  7.1 0.0 copy-start.12
  7.1 0.8 %copy-done.12 = bf16[256,128]{1,0:T(8,128)(2,1)S(1)} copy-done((bf16[256,128]{1,0:T(8,128)(2,1)S(1)}, bf16[256,128]{1,0:T(8,128)(2,1)}, u32[]{:S(2)}) %copy-start.12) | copy-done | bytes 65560
  8.0 0.0 copy-start.13
  8.0 0.7 %copy-done.13 = s32[32]{0:T(128)S(1)} copy-done((s32[32]{0:T(128)S(1)}, s32[32]{0:T(128)}, u32[]{:S(2)}) %copy-start.13) | copy-done | bytes 152
  8.6 0.0 copy-start.1
  8.6 0.0 copy-start.3
  8.6 0.0 copy-start.5
  8.6 0.0 copy-start.7
  8.6 0.0 copy-start.9
  8.7 26.2 %exchange.1.pieces = bf16[16,3,32,128]{3,2,1,0:T(8,128)(2,1)S(1)} custom-call(s32[32]{0:T(128)S(1)} %copy-done.13, bf16[256,512]{1,0:T(8,128)(2,1)S(1)} %copy-done, bf16[256,512]{1,0:T(8,128)(2,1)S(1)} %copy-done.8, bf16[256,512]{1,0:T(8,128)(2,1)S(1)} %copy-done.2, bf16[256,512]{1,0:T(8,128)(2,1)S(1)} %copy-done.4, f32[48,512]{1,0:T(8,128)S(1)} %copy-done.11, ...), custom_call_target="tpu_custom_call" | custom-call | tf_op jit(solution)/shard_map/exchange/pallas_call | solution.py:217
  34.8 0.0 copy-done.1
  34.8 0.0 copy-done.3
  34.8 0.0 copy-done.5
  34.9 0.0 copy-done.7
  34.9 0.0 copy-done.9
  34.9 1.2 %finish.1 = (bf16[256,512]{1,0:T(8,128)(2,1)}, bf16[256,512]{1,0:T(8,128)(2,1)}, bf16[256,512]{1,0:T(8,128)(2,1)}, f32[48,512]{1,0:T(8,128)}) custom-call(bf16[256,512]{1,0:T(8,128)(2,1)S(1)} %copy-done.1, bf16[256,512]{1,0:T(8,128)(2,1)S(1)} %copy-done.9, bf16[256,512]{1,0:T(8,128)(2,1)S(1)} %copy-done.3, bf16[256,512]{1,0:T(8,128)(2,1)S(1)} %copy-done.5, ...), custom_call_target="tpu_custom_call" | custom-call | tf_op jit(solution)/shard_map/finish/pallas_call | solution.py:240
Async XLA Ops:
  0.6 1.0 %copy-start = (bf16[256,512]{1,0:T(8,128)(2,1)S(1)}, bf16[256,512]{1,0:T(8,128)(2,1)}, u32[]{:S(2)}) copy-start(bf16[256,512]{1,0:T(8,128)(2,1)} %grad.3) | copy-start | bytes 786436
  1.6 0.9 %copy-start.2 = (bf16[256,512]{1,0:T(8,128)(2,1)S(1)}, bf16[256,512]{1,0:T(8,128)(2,1)}, u32[]{:S(2)}) copy-start(bf16[256,512]{1,0:T(8,128)(2,1)} %key.3) | copy-start | bytes 786436
  2.5 0.9 %copy-start.4 = (bf16[256,512]{1,0:T(8,128)(2,1)S(1)}, bf16[256,512]{1,0:T(8,128)(2,1)}, u32[]{:S(2)}) copy-start(bf16[256,512]{1,0:T(8,128)(2,1)} %value.3) | copy-start | bytes 786436
  3.5 0.9 %copy-start.6 = (bf16[256,256]{1,0:T(8,128)(2,1)S(1)}, bf16[256,256]{1,0:T(8,128)(2,1)}, u32[]{:S(2)}) copy-start(bf16[256,256]{1,0:T(8,128)(2,1)} %constant.8.clone.eye) | copy-start | bytes 393220
  4.4 0.9 %copy-start.8 = (bf16[256,512]{1,0:T(8,128)(2,1)S(1)}, bf16[256,512]{1,0:T(8,128)(2,1)}, u32[]{:S(2)}) copy-start(bf16[256,512]{1,0:T(8,128)(2,1)} %query.1) | copy-start | bytes 786436
  5.3 0.9 %copy-start.10 = (bf16[256,256]{1,0:T(8,128)(2,1)S(1)}, bf16[256,256]{1,0:T(8,128)(2,1)}, u32[]{:S(2)}) copy-start(bf16[256,256]{1,0:T(8,128)(2,1)} %constant.6.clone.forward) | copy-start | bytes 393220
  6.2 0.9 %copy-start.11 = (f32[48,512]{1,0:T(8,128)S(1)}, f32[48,512]{1,0:T(8,128)}, u32[]{:S(2)}) copy-start(f32[48,512]{1,0:T(8,128)} %taps.1) | copy-start | bytes 294916
  7.1 0.8 %copy-start.12 = (bf16[256,128]{1,0:T(8,128)(2,1)S(1)}, bf16[256,128]{1,0:T(8,128)(2,1)}, u32[]{:S(2)}) copy-start(bf16[256,128]{1,0:T(8,128)(2,1)} %constant.7.clone.back) | copy-start | bytes 196612
  8.0 0.7 %copy-start.13 = (s32[32]{0:T(128)S(1)}, s32[32]{0:T(128)}, u32[]{:S(2)}) copy-start(s32[32]{0:T(128)} %table.1) | copy-start | bytes 388
  8.6 26.2 %copy-start.1 = (bf16[256,512]{1,0:T(8,128)(2,1)S(1)}, bf16[256,512]{1,0:T(8,128)(2,1)}, u32[]{:S(2)}) copy-start(bf16[256,512]{1,0:T(8,128)(2,1)} %grad.3) | copy-start | bytes 786436
  8.6 26.2 %copy-start.3 = (bf16[256,512]{1,0:T(8,128)(2,1)S(1)}, bf16[256,512]{1,0:T(8,128)(2,1)}, u32[]{:S(2)}) copy-start(bf16[256,512]{1,0:T(8,128)(2,1)} %key.3) | copy-start | bytes 786436
  8.6 26.2 %copy-start.5 = (bf16[256,512]{1,0:T(8,128)(2,1)S(1)}, bf16[256,512]{1,0:T(8,128)(2,1)}, u32[]{:S(2)}) copy-start(bf16[256,512]{1,0:T(8,128)(2,1)} %value.3) | copy-start | bytes 786436
  8.6 26.2 %copy-start.7 = (bf16[256,256]{1,0:T(8,128)(2,1)S(1)}, bf16[256,256]{1,0:T(8,128)(2,1)}, u32[]{:S(2)}) copy-start(bf16[256,256]{1,0:T(8,128)(2,1)} %constant.8.clone.eye) | copy-start | bytes 393220
  8.6 26.2 %copy-start.9 = (bf16[256,512]{1,0:T(8,128)(2,1)S(1)}, bf16[256,512]{1,0:T(8,128)(2,1)}, u32[]{:S(2)}) copy-start(bf16[256,512]{1,0:T(8,128)(2,1)} %conv.1) | copy-start | bytes 786436

commit v2 on v1

v2 whole, which is shorter than its diff:
```python
import functools

import jax
import jax.numpy as jnp
import numpy as np
from jax import lax
from jax.experimental import pallas as pl
from jax.experimental.pallas import tpu as pltpu
from jax.sharding import PartitionSpec as P

BLOCK = 128
LAG_BLOCKS = 6
SPAN = 2 * BLOCK
RANKS = 16
SLOTS = 2 * RANKS
MESH = pl.DeviceIdType.MESH
F32 = jnp.float32
BF16 = jnp.bfloat16
NT = (((1,), (1,)), ((), ()))


def tables():
    time = np.arange(SPAN)[:, None]
    bins = np.arange(BLOCK)[None, :] + 0.5
    angles = 2.0 * np.pi * time * bins / SPAN
    forward = np.concatenate([np.cos(angles), -np.sin(angles)], 1)
    back = np.concatenate([np.cos(angles[:BLOCK]).T, -np.sin(angles[:BLOCK]).T], 0) * (2.0 / SPAN)
    return jnp.asarray(forward, BF16), jnp.asarray(back, BF16)


def dot(left, right):
    return jnp.dot(left, right, preferred_element_type=F32)


def flip(eye, rows):
    return lax.dot_general(eye, rows, NT, preferred_element_type=F32)


def peer(me, offset):
    dx, dy, dc = offset
    x = lax.rem(lax.div(me, 4) + dx, 4)
    y = lax.rem(lax.rem(lax.div(me, 2), 2) + dy, 2)
    c = lax.rem(lax.rem(me, 2) + dc, 2)
    return (x * 2 + y) * 2 + c


OFFSETS = sorted(
    [(dx, dy, dc) for dx in range(4) for dy in range(2) for dc in range(2)][1:],
    key=lambda o: -(min(o[0], 4 - o[0]) + 2 * o[1] + o[2]),
)


CHUNKS = 4
ROWS = 8


def load_all(pairs, sems):
    loads = []
    for i, (source, target) in enumerate(pairs):
        load = pltpu.make_async_copy(source, target, sems.at[i])
        load.start()
        loads.append(load)
    return loads


def unit_matrix(size):
    row = lax.broadcasted_iota(jnp.int32, (size, size), 0)
    column = lax.broadcasted_iota(jnp.int32, (size, size), 1)
    return jnp.where(row == column, 1.0, 0.0).astype(BF16)


def exchange_kernel(
    table_in, grad_in, query_in, key_in, value_in, taps_in, forward_in, back_in, out,
    table, inverse, grad, query, key, value, taps, forward, back,
    send_f, recv_f, send_a, recv_a, send_b, spec_w, spec_u, spec_h, spec_d, spec_f, lag_rows,
    load_sems, f_send, f_recv, a_send, a_recv, b_send, b_recv, own_sems,
):
    me = lax.axis_index("ctx")
    loads = load_all(
        ((taps_in, taps), (grad_in, grad), (query_in, query), (key_in, key), (value_in, value),
         (forward_in, forward), (back_in, back), (table_in, table)),
        load_sems,
    )
    peers = [peer(me, offset) for offset in OFFSETS]
    barrier = pltpu.get_barrier_semaphore()
    for to in peers:
        pl.semaphore_signal(barrier, inc=1, device_id={"ctx": to}, device_id_type=MESH)

    def send(source, target, send_sems, recv_sems):
        copies = []
        for i, to in enumerate(peers):
            copy = pltpu.make_async_remote_copy(
                source(to), target, send_sems.at[i], recv_sems.at[i],
                device_id={"ctx": to}, device_id_type=MESH,
            )
            copy.start()
            copies.append(copy)
        return copies

    unit = unit_matrix(SPAN)
    lane = lax.broadcasted_iota(jnp.int32, (16, BLOCK), 1)
    lower = lane < 64
    lags = taps.shape[0]
    loads[0].wait()
    padded = jnp.concatenate([taps[...].astype(BF16), jnp.zeros((BLOCK - lags, taps.shape[1]), BF16)], 0)
    for half in range(2):
        turned = flip(unit, padded[:, half * SPAN:(half + 1) * SPAN])
        for piece in range(8):
            rows = turned[piece * 32:(piece + 1) * 32]
            packed = jnp.where(lower, rows[:16], pltpu.roll(rows[16:], 64, 1))
            send_f[half * 8 + piece] = packed.astype(BF16)

    for which, (left, right) in enumerate(((grad, query), (key, value))):
        loads[1 + 2 * which].wait()
        loads[2 + 2 * which].wait()
        product = (left[...].astype(F32) * right[...].astype(F32)).astype(BF16)
        for half in range(2):
            turned = flip(unit, product[:, half * SPAN:(half + 1) * SPAN]).reshape(8, CHUNKS, ROWS, SPAN)
            for piece in range(8):
                for c in range(CHUNKS):
                    rows = turned[piece, c]
                    send_a[c, half * 8 + piece, which] = jnp.concatenate(
                        [rows[:, :BLOCK], rows[:, BLOCK:]], 0
                    ).astype(BF16)

    pl.semaphore_wait(barrier, len(OFFSETS))
    copies_f = send(lambda to: send_f.at[to], recv_f.at[me], f_send, f_recv)
    copies_a = [
        send(lambda to: send_a.at[c, to], recv_a.at[c, me], a_send.at[c], a_recv.at[c])
        for c in range(CHUNKS)
    ]
    own_f = pltpu.make_async_copy(send_f.at[me], recv_f.at[me], own_sems.at[0])
    own_f.start()
    own_a = pltpu.make_async_copy(send_a.at[:, me], recv_a.at[:, me], own_sems.at[1])
    own_a.start()

    def slot_of(p, carry):
        found = jnp.int32(0)
        for s in range(SLOTS):
            found = jnp.where(table[s] == p, s, found)
        inverse[p] = found
        return carry

    loads[7].wait()
    lax.fori_loop(0, SLOTS, slot_of, 0)
    own_f.wait()
    own_a.wait()
    loads[5].wait()
    loads[6].wait()

    for copy in copies_f:
        copy.wait_recv()
    order = [[jnp.zeros((16, BLOCK), F32) for _ in range(2)] for _ in range(LAG_BLOCKS)]
    for src in range(RANKS):
        first, shift = divmod(src * lags, BLOCK)
        packed = recv_f[src].astype(F32)
        for part in range(2):
            turn = (shift + 64 * part) % BLOCK
            rows = pltpu.roll(packed, turn, 1) if turn else packed
            inside = (lane >= shift) & (lane < shift + lags)
            order[first][part] = jnp.where(inside, rows, order[first][part])
            if shift + lags > BLOCK:
                order[first + 1][part] = jnp.where(lane < shift + lags - BLOCK, rows, order[first + 1][part])
    taps_in_order = jnp.concatenate([part for parts in order for part in parts], 0).astype(BF16)
    spec_h[...] = dot(taps_in_order, forward[:BLOCK]).reshape(LAG_BLOCKS, 32, SPAN)

    copies_b = []
    for c in range(CHUNKS):
        for copy in copies_a[c]:
            copy.wait_recv()
        rows_w = recv_a[c, :, 0].reshape(RANKS * 2 * ROWS, BLOCK)
        rows_u = recv_a[c, :, 1].reshape(RANKS * 2 * ROWS, BLOCK)
        spec_w[:, :, :SPAN] = dot(rows_w, forward[:BLOCK]).reshape(SLOTS, ROWS, SPAN)
        spec_w[:, :, SPAN:] = dot(rows_w, forward[BLOCK:]).reshape(SLOTS, ROWS, SPAN)
        spec_u[...] = dot(rows_u, forward[:BLOCK]).reshape(SLOTS, ROWS, SPAN)

        def window(p):
            slot = inverse[p]
            re = spec_w[slot, :, :BLOCK]
            im = spec_w[slot, :, BLOCK:SPAN]
            if p + 1 < SLOTS:
                later = inverse[p + 1]
                re = re + spec_w[later, :, SPAN:SPAN + BLOCK]
                im = im + spec_w[later, :, SPAN + BLOCK:]
            return re, im

        group = slice(c * ROWS, (c + 1) * ROWS)
        h = [(spec_h[m, group, :BLOCK], spec_h[m, group, BLOCK:]) for m in range(LAG_BLOCKS)]
        f = [None] * LAG_BLOCKS
        windows = [window(p) for p in range(LAG_BLOCKS - 1)]
        for p in range(SLOTS):
            if p + LAG_BLOCKS - 1 < SLOTS:
                windows.append(window(p + LAG_BLOCKS - 1))
            slot = inverse[p]
            u_re, u_im = spec_u[slot, :, :BLOCK], spec_u[slot, :, BLOCK:]
            d = None
            for m in range(min(LAG_BLOCKS, SLOTS - p)):
                v_re, v_im = windows[p + m]
                h_re, h_im = h[m]
                term_f = (u_re * v_re + u_im * v_im, u_re * v_im - u_im * v_re)
                term_d = (h_re * v_re + h_im * v_im, h_re * v_im - h_im * v_re)
                f[m] = term_f if f[m] is None else (f[m][0] + term_f[0], f[m][1] + term_f[1])
                d = term_d if d is None else (d[0] + term_d[0], d[1] + term_d[1])
            windows[p] = None
            spec_d[p, :, :BLOCK] = d[0]
            spec_d[p, :, BLOCK:] = d[1]
        for m in range(LAG_BLOCKS):
            spec_f[m, :, :BLOCK] = f[m][0]
            spec_f[m, :, BLOCK:] = f[m][1]

        rows_d = jnp.concatenate([spec_d[table[s]] for s in range(SLOTS)], 0).astype(BF16)
        send_b[c] = dot(rows_d, back[...]).astype(BF16).reshape(RANKS, 2 * ROWS, BLOCK)
        copies_b += send(lambda to: send_b.at[c, to], out.at[c, me], b_send.at[c], b_recv.at[c])
        rows_f = spec_f[...].reshape(LAG_BLOCKS * ROWS, SPAN).astype(BF16)
        lag_rows[:, group] = dot(rows_f, back[...]).reshape(LAG_BLOCKS, ROWS, BLOCK)

    scale = float((SLOTS * BLOCK) ** -0.5)
    for to in range(RANKS):
        first, shift = divmod(to * lags, BLOCK)
        parts = []
        for part in range(2):
            turn = (64 * part - shift) % BLOCK
            rows = lag_rows[first, part * 16:(part + 1) * 16]
            rows = pltpu.roll(rows, turn, 1) if turn else rows
            if shift + lags > BLOCK:
                later = pltpu.roll(lag_rows[first + 1, part * 16:(part + 1) * 16], turn, 1)
                rows = jnp.where((lane & 63) < BLOCK - shift, rows, later)
            parts.append(rows)
        send_b[CHUNKS, to] = (jnp.where(lower, parts[0], parts[1]) * scale).astype(BF16)
    copies_b += send(
        lambda to: send_b.at[CHUNKS, to], out.at[CHUNKS, me], b_send.at[CHUNKS], b_recv.at[CHUNKS]
    )
    own_b = pltpu.make_async_copy(send_b.at[:, me], out.at[:, me], own_sems.at[0])
    own_b.start()
    own_b.wait()
    for copies in [copies_f] + copies_a:
        for copy in copies:
            copy.wait_send()
    for copy in copies_b:
        copy.wait()


def finish_kernel(grad, conv, key, value, pieces, q_out, k_out, v_out, f_out):
    q_out[...] = (grad[...].astype(F32) * conv[...].astype(F32)).astype(BF16)
    unit = unit_matrix(BLOCK)
    channels = grad.shape[1]
    chunks = pieces[:CHUNKS].astype(F32).reshape(CHUNKS, RANKS, 2, ROWS, BLOCK)
    for b in range(2):
        rows = slice(b * BLOCK, (b + 1) * BLOCK)
        piece = jnp.stack([chunks[c, :, b] for c in range(CHUNKS)], 1)
        turned = flip(unit, piece.reshape(channels, BLOCK).astype(BF16))
        k_out[rows] = (turned * value[rows].astype(F32)).astype(BF16)
        v_out[rows] = (turned * key[rows].astype(F32)).astype(BF16)
    packed = pieces[CHUNKS].astype(F32).reshape(RANKS * 16, BLOCK)
    upper = pltpu.roll(packed, 64, 1).reshape(RANKS, 16, BLOCK)
    both = jnp.stack([packed.reshape(RANKS, 16, BLOCK), upper], 1)
    f_out[...] = flip(unit[:f_out.shape[0]], both.reshape(channels, BLOCK).astype(BF16))


def on_device(out_grad, query_rows, key_rows, value_rows, conv_rows, long_filter, block_table):
    forward, back = tables()
    vmem = pl.BlockSpec(memory_space=pltpu.VMEM)
    units = (CHUNKS + 1, RANKS, 16, BLOCK)
    sums = pltpu.VMEM((LAG_BLOCKS, ROWS, SPAN), F32)
    dma = pltpu.SemaphoreType.DMA
    rows = jax.ShapeDtypeStruct(out_grad.shape, BF16)
    operands = (block_table, out_grad, query_rows, key_rows, value_rows, long_filter, forward, back)
    pieces = pl.pallas_call(
        exchange_kernel,
        name="exchange",
        out_shape=jax.ShapeDtypeStruct(units, BF16),
        in_specs=[pl.BlockSpec(memory_space=pltpu.HBM)] * 8,
        out_specs=vmem,
        scratch_shapes=[
            pltpu.SMEM((SLOTS,), jnp.int32),
            pltpu.SMEM((SLOTS,), jnp.int32),
            pltpu.VMEM(rows.shape, BF16),
            pltpu.VMEM(rows.shape, BF16),
            pltpu.VMEM(rows.shape, BF16),
            pltpu.VMEM(rows.shape, BF16),
            pltpu.VMEM(long_filter.shape, F32),
            pltpu.VMEM(forward.shape, BF16),
            pltpu.VMEM(back.shape, BF16),
            pltpu.VMEM((RANKS, 16, BLOCK), BF16),
            pltpu.VMEM((RANKS, 16, BLOCK), BF16),
            pltpu.VMEM((CHUNKS, RANKS, 2, 16, BLOCK), BF16),
            pltpu.VMEM((CHUNKS, RANKS, 2, 16, BLOCK), BF16),
            pltpu.VMEM(units, BF16),
            pltpu.VMEM((SLOTS, ROWS, 2 * SPAN), F32),
            pltpu.VMEM((SLOTS, ROWS, SPAN), F32),
            pltpu.VMEM((LAG_BLOCKS, 32, SPAN), F32),
            pltpu.VMEM((SLOTS, ROWS, SPAN), F32),
            sums,
            pltpu.VMEM((LAG_BLOCKS, 32, BLOCK), F32),
            dma((8,)), dma((15,)), dma((15,)), dma((CHUNKS, 15)), dma((CHUNKS, 15)),
            dma((CHUNKS + 1, 15)), dma((CHUNKS + 1, 15)), dma((2,)),
        ],
        compiler_params=pltpu.CompilerParams(
            collective_id=0, has_side_effects=True, vmem_limit_bytes=40 * 1024 * 1024
        ),
    )(*(pltpu.with_memory_space_constraint(x, pltpu.HBM) for x in operands))
    return pl.pallas_call(
        finish_kernel,
        name="finish",
        out_shape=(rows, rows, rows, jax.ShapeDtypeStruct(long_filter.shape, F32)),
        in_specs=[vmem] * 5,
        out_specs=[vmem] * 4,
        compiler_params=pltpu.CompilerParams(vmem_limit_bytes=40 * 1024 * 1024),
    )(out_grad, conv_rows, key_rows, value_rows, pieces)


def solution(mesh):
    rows = P("ctx", "tp")
    return jax.shard_map(
        on_device, mesh=mesh, in_specs=(rows,) * 6 + (P(),), out_specs=(rows,) * 4, check_vma=False
    )
```

time: 36.4 us -> 27.3 us (0.75)
  local copies, waits for them, and re-layouts: 8 us -> 0.02 us
  Pallas kernels: 27.3 us -> 26.4 us
    unnamed x28 -> x8, local copies, waits for them, and re-layouts: 8 us -> 0.02 us
    pallas_call x1, Pallas kernels: 26.2 us -> 25.3 us  [on_device(): pl.pallas_call(exchange_kernel, name='exchange', out_shape=jax.ShapeDtype...]
where the time goes in v2:
time: 27.3 us; the launch traced here: 27.2 us
  Pallas kernels  26.4 us (97%)
  between operations  0.7 us (3%)
    pallas_call x1, Pallas kernels, on_device(): pl.pallas_call(exchange_kernel, name='exchange', out_shape=jax.ShapeDtype...  25.3 us
    pallas_call x1, Pallas kernels, on_device(): pl.pallas_call(finish_kernel, name='finish', out_shape=(rows, rows, rows,...  1.16 us

profile of v2, /device:TPU:1, one launch (start us, length us, event | category | flops | bytes accessed | tf_op | source)
XLA Modules:
  0.0 27.2 jit_solution(17923575839643635770)
XLA Ops:
  0.6 0.0 copy-start.2
  0.6 0.0 copy-start.1
  0.7 0.0 copy-start
  0.7 0.0 copy-start.3
  0.7 25.3 %exchange.1.pieces = bf16[5,16,16,128]{3,2,1,0:T(8,128)(2,1)S(1)} custom-call(s32[32]{0:T(128)} %table_in.1, bf16[256,512]{1,0:T(8,128)(2,1)} %grad.1, bf16[256,512]{1,0:T(8,128)(2,1)} %query_in.1, bf16[256,512]{1,0:T(8,128)(2,1)} %key.1, bf16[256,512]{1,0:T(8,128)(2,1)} %value.1, f32[48,512]{1,0:T(8,128)} %taps_in.1, ...), custom_call_target="tpu_custom_call" | custom-call | tf_op jit(solution)/shard_map/exchange/pallas_call | solution.py:268
  25.9 0.0 copy-done.2
  26.0 0.0 copy-done.1
  26.0 0.0 copy-done
  26.0 0.0 copy-done.3
  26.0 1.2 %finish.1 = (bf16[256,512]{1,0:T(8,128)(2,1)}, bf16[256,512]{1,0:T(8,128)(2,1)}, bf16[256,512]{1,0:T(8,128)(2,1)}, f32[48,512]{1,0:T(8,128)}) custom-call(bf16[256,512]{1,0:T(8,128)(2,1)S(1)} %copy-done, bf16[256,512]{1,0:T(8,128)(2,1)S(1)} %copy-done.3, bf16[256,512]{1,0:T(8,128)(2,1)S(1)} %copy-done.1, bf16[256,512]{1,0:T(8,128)(2,1)S(1)} %copy-done.2, ...), custom_call_target="tpu_custom_call" | custom-call | tf_op jit(solution)/shard_map/finish/pallas_call | solution.py:302
Async XLA Ops:
  0.6 25.3 %copy-start.2 = (bf16[256,512]{1,0:T(8,128)(2,1)S(1)}, bf16[256,512]{1,0:T(8,128)(2,1)}, u32[]{:S(2)}) copy-start(bf16[256,512]{1,0:T(8,128)(2,1)} %value.1) | copy-start | bytes 786436
  0.6 25.3 %copy-start.1 = (bf16[256,512]{1,0:T(8,128)(2,1)S(1)}, bf16[256,512]{1,0:T(8,128)(2,1)}, u32[]{:S(2)}) copy-start(bf16[256,512]{1,0:T(8,128)(2,1)} %key.1) | copy-start | bytes 786436
  0.7 25.3 %copy-start = (bf16[256,512]{1,0:T(8,128)(2,1)S(1)}, bf16[256,512]{1,0:T(8,128)(2,1)}, u32[]{:S(2)}) copy-start(bf16[256,512]{1,0:T(8,128)(2,1)} %grad.1) | copy-start | bytes 786436
  0.7 25.3 %copy-start.3 = (bf16[256,512]{1,0:T(8,128)(2,1)S(1)}, bf16[256,512]{1,0:T(8,128)(2,1)}, u32[]{:S(2)}) copy-start(bf16[256,512]{1,0:T(8,128)(2,1)} %conv.1) | copy-start | bytes 786436

commit v3 on v2

v3 whole, which is shorter than its diff:
```python
import functools

import jax
import jax.numpy as jnp
import numpy as np
from jax import lax
from jax.experimental import pallas as pl
from jax.experimental.pallas import tpu as pltpu
from jax.sharding import PartitionSpec as P

BLOCK = 128
LAG_BLOCKS = 6
SPAN = 2 * BLOCK
RANKS = 16
SLOTS = 2 * RANKS
MESH = pl.DeviceIdType.MESH
F32 = jnp.float32
BF16 = jnp.bfloat16
NT = (((1,), (1,)), ((), ()))


def tables():
    time = np.arange(SPAN)[:, None]
    bins = np.arange(BLOCK)[None, :] + 0.5
    angles = 2.0 * np.pi * time * bins / SPAN
    forward = np.concatenate([np.cos(angles), -np.sin(angles)], 1)
    back = np.concatenate([np.cos(angles[:BLOCK]).T, -np.sin(angles[:BLOCK]).T], 0) * (2.0 / SPAN)
    return jnp.asarray(forward, BF16), jnp.asarray(back, BF16)


def dot(left, right):
    return jnp.dot(left, right, preferred_element_type=F32)


def flip(eye, rows):
    return lax.dot_general(eye, rows, NT, preferred_element_type=F32)


def peer(me, offset):
    dx, dy, dc = offset
    x = lax.rem(lax.div(me, 4) + dx, 4)
    y = lax.rem(lax.rem(lax.div(me, 2), 2) + dy, 2)
    c = lax.rem(lax.rem(me, 2) + dc, 2)
    return (x * 2 + y) * 2 + c


OFFSETS = (
    (2, 1, 1), (2, 1, 0), (1, 1, 1), (3, 1, 0), (3, 1, 1), (1, 1, 0), (2, 0, 1), (0, 1, 0),
    (0, 1, 1), (2, 0, 0), (1, 0, 1), (3, 0, 0), (3, 0, 1), (1, 0, 0), (0, 0, 1),
)


CHUNKS = 4
ROWS = 8


def load_all(pairs, sems):
    loads = []
    for i, (source, target) in enumerate(pairs):
        load = pltpu.make_async_copy(source, target, sems.at[i])
        load.start()
        loads.append(load)
    return loads


def unit_matrix(size):
    row = lax.broadcasted_iota(jnp.int32, (size, size), 0)
    column = lax.broadcasted_iota(jnp.int32, (size, size), 1)
    return jnp.where(row == column, 1.0, 0.0).astype(BF16)


def exchange_kernel(
    table_in, grad_in, query_in, key_in, value_in, taps_in, forward_in, back_in, out,
    table, inverse, grad, query, key, value, taps, forward, back,
    send_w, recv_w, send_u, recv_u, send_b, spec_w, spec_v, spec_u, spec_h, spec_d, spec_f,
    load_sems, w_send, w_recv, u_send, u_recv, d_send, d_recv, f_send, f_recv, own_sems,
):
    me = lax.axis_index("ctx")
    loads = load_all(
        ((taps_in, taps), (grad_in, grad), (query_in, query), (key_in, key), (value_in, value),
         (forward_in, forward), (back_in, back), (table_in, table)),
        load_sems,
    )
    peers = [peer(me, offset) for offset in OFFSETS]
    barrier = pltpu.get_barrier_semaphore()
    for to in peers:
        pl.semaphore_signal(barrier, inc=1, device_id={"ctx": to}, device_id_type=MESH)

    def send(source, target, send_sems, recv_sems):
        copies = []
        for i, to in enumerate(peers):
            copy = pltpu.make_async_remote_copy(
                source(to), target, send_sems.at[i], recv_sems.at[i],
                device_id={"ctx": to}, device_id_type=MESH,
            )
            copy.start()
            copies.append(copy)
        return copies

    def keep(source, target, i):
        copy = pltpu.make_async_copy(source, target, own_sems.at[i])
        copy.start()
        return copy

    unit = unit_matrix(SPAN)
    lane = lax.broadcasted_iota(jnp.int32, (16, BLOCK), 1)
    lower = lane < 64
    lags = taps.shape[0]
    loads[0].wait()
    padded = jnp.concatenate([taps[...].astype(BF16), jnp.zeros((BLOCK - lags, taps.shape[1]), BF16)], 0)
    for half in range(2):
        turned = flip(unit, padded[:, half * SPAN:(half + 1) * SPAN])
        for piece in range(8):
            rows = turned[piece * 32:(piece + 1) * 32]
            packed = jnp.where(lower, rows[:16], pltpu.roll(rows[16:], 64, 1))
            send_w[half * 8 + piece, CHUNKS] = packed.astype(BF16)

    def cut(left, right, pieces):
        product = (left[...].astype(F32) * right[...].astype(F32)).astype(BF16)
        for half in range(2):
            turned = flip(unit, product[:, half * SPAN:(half + 1) * SPAN]).reshape(8, CHUNKS, ROWS, SPAN)
            for piece in range(8):
                for c in range(CHUNKS):
                    rows = turned[piece, c]
                    pieces[half * 8 + piece, c] = jnp.concatenate(
                        [rows[:, :BLOCK], rows[:, BLOCK:]], 0
                    ).astype(BF16)

    loads[1].wait()
    loads[2].wait()
    cut(grad, query, send_w)
    pl.semaphore_wait(barrier, len(OFFSETS))
    copies_w = send(lambda to: send_w.at[to], recv_w.at[me], w_send, w_recv)
    own_w = keep(send_w.at[me], recv_w.at[me], 0)
    loads[3].wait()
    loads[4].wait()
    cut(key, value, send_u)
    copies_u = send(lambda to: send_u.at[to], recv_u.at[me], u_send, u_recv)
    own_u = keep(send_u.at[me], recv_u.at[me], 1)

    def slot_of(p, carry):
        found = jnp.int32(0)
        for s in range(SLOTS):
            found = jnp.where(table[s] == p, s, found)
        inverse[p] = found
        return carry

    for load in loads[5:]:
        load.wait()
    lax.fori_loop(0, SLOTS, slot_of, 0)
    spec_v[:, SLOTS:] = jnp.zeros((CHUNKS, LAG_BLOCKS - 1, ROWS, SPAN), F32)
    spec_f[...] = jnp.zeros_like(spec_f)
    own_w.wait()
    own_u.wait()
    for copy in copies_w:
        copy.wait_recv()

    order = [[jnp.zeros((16, BLOCK), F32) for _ in range(2)] for _ in range(LAG_BLOCKS)]
    for src in range(RANKS):
        first, shift = divmod(src * lags, BLOCK)
        packed = recv_w[src, CHUNKS].astype(F32)
        for part in range(2):
            turn = (shift + 64 * part) % BLOCK
            rows = pltpu.roll(packed, turn, 1) if turn else packed
            inside = (lane >= shift) & (lane < shift + lags)
            order[first][part] = jnp.where(inside, rows, order[first][part])
            if shift + lags > BLOCK:
                order[first + 1][part] = jnp.where(lane < shift + lags - BLOCK, rows, order[first + 1][part])
    taps_in_order = jnp.concatenate([part for parts in order for part in parts], 0).astype(BF16)
    spec_h[...] = dot(taps_in_order, forward[:BLOCK]).reshape(LAG_BLOCKS, 32, SPAN)

    for c in range(CHUNKS):
        rows_w = recv_w[:, c].reshape(RANKS * 2 * ROWS, BLOCK)
        spec_w[c, :, :, :SPAN] = dot(rows_w, forward[:BLOCK]).reshape(SLOTS, ROWS, SPAN)
        spec_w[c, :, :, SPAN:] = dot(rows_w, forward[BLOCK:]).reshape(SLOTS, ROWS, SPAN)

    for c in range(CHUNKS):
        def window(p):
            slot = inverse[p]
            re = spec_w[c, slot, :, :BLOCK]
            im = spec_w[c, slot, :, BLOCK:SPAN]
            if p + 1 < SLOTS:
                later = inverse[p + 1]
                re = re + spec_w[c, later, :, SPAN:SPAN + BLOCK]
                im = im + spec_w[c, later, :, SPAN + BLOCK:]
            spec_v[c, p, :, :BLOCK] = re
            spec_v[c, p, :, BLOCK:] = im
            return re, im

        group = slice(c * ROWS, (c + 1) * ROWS)
        h = [(spec_h[m, group, :BLOCK], spec_h[m, group, BLOCK:]) for m in range(LAG_BLOCKS)]
        windows = [window(p) for p in range(LAG_BLOCKS - 1)]
        for p in range(SLOTS):
            if p + LAG_BLOCKS - 1 < SLOTS:
                windows.append(window(p + LAG_BLOCKS - 1))
            d = None
            for m in range(min(LAG_BLOCKS, SLOTS - p)):
                v_re, v_im = windows[p + m]
                h_re, h_im = h[m]
                term = (h_re * v_re + h_im * v_im, h_re * v_im - h_im * v_re)
                d = term if d is None else (d[0] + term[0], d[1] + term[1])
            windows[p] = None
            spec_d[c, p, :, :BLOCK] = d[0]
            spec_d[c, p, :, BLOCK:] = d[1]

        rows_d = jnp.concatenate([spec_d[c, table[s]] for s in range(SLOTS)], 0).astype(BF16)
        send_b[:, c] = dot(rows_d, back[...]).astype(BF16).reshape(RANKS, 2 * ROWS, BLOCK)
    copies_d = send(
        lambda to: send_b.at[to, pl.ds(0, CHUNKS)], out.at[me, pl.ds(0, CHUNKS)], d_send, d_recv
    )

    sources = [me] + [peer(me, ((4 - dx) % 4, dy, dc)) for dx, dy, dc in OFFSETS]
    for start in range(0, RANKS, 4):
        for copy in copies_u[max(start - 1, 0):start + 3]:
            copy.wait_recv()
        batch = sources[start:start + 4]
        rows_u = jnp.concatenate([recv_u[src].reshape(CHUNKS * 16, BLOCK) for src in batch], 0)
        spec_u[...] = dot(rows_u, forward[:BLOCK]).reshape(4, CHUNKS, 2, ROWS, SPAN)
        for c in range(CHUNKS):
            f = [(spec_f[c, m, :, :BLOCK], spec_f[c, m, :, BLOCK:]) for m in range(LAG_BLOCKS)]
            for i, src in enumerate(batch):
                for b in range(2):
                    p = table[2 * src + b]
                    u_re, u_im = spec_u[i, c, b, :, :BLOCK], spec_u[i, c, b, :, BLOCK:]
                    for m in range(LAG_BLOCKS):
                        v_re, v_im = spec_v[c, p + m, :, :BLOCK], spec_v[c, p + m, :, BLOCK:]
                        f[m] = (
                            f[m][0] + (u_re * v_re + u_im * v_im),
                            f[m][1] + (u_re * v_im - u_im * v_re),
                        )
            for m in range(LAG_BLOCKS):
                spec_f[c, m, :, :BLOCK] = f[m][0]
                spec_f[c, m, :, BLOCK:] = f[m][1]
    rows_f = spec_f[...].reshape(CHUNKS * LAG_BLOCKS * ROWS, SPAN).astype(BF16)
    scale = float((SLOTS * BLOCK) ** -0.5)
    lagged = (dot(rows_f, back[...]) * scale).reshape(CHUNKS, LAG_BLOCKS, ROWS, BLOCK)
    lag_rows = [
        [jnp.concatenate([lagged[2 * part, m], lagged[2 * part + 1, m]], 0) for part in range(2)]
        for m in range(LAG_BLOCKS)
    ]
    for to in range(RANKS):
        first, shift = divmod(to * lags, BLOCK)
        parts = []
        for part in range(2):
            turn = (64 * part - shift) % BLOCK
            rows = lag_rows[first][part]
            rows = pltpu.roll(rows, turn, 1) if turn else rows
            if shift + lags > BLOCK:
                later = pltpu.roll(lag_rows[first + 1][part], turn, 1)
                rows = jnp.where((lane & 63) < BLOCK - shift, rows, later)
            parts.append(rows)
        send_b[to, CHUNKS] = jnp.where(lower, parts[0], parts[1]).astype(BF16)
    copies_f = send(lambda to: send_b.at[to, CHUNKS], out.at[me, CHUNKS], f_send, f_recv)
    own_b = keep(send_b.at[me], out.at[me], 0)
    for copy in copies_w + copies_u:
        copy.wait_send()
    own_b.wait()
    for copy in copies_d + copies_f:
        copy.wait()


def finish_kernel(grad, conv, key, value, pieces, q_out, k_out, v_out, f_out):
    q_out[...] = (grad[...].astype(F32) * conv[...].astype(F32)).astype(BF16)
    unit = unit_matrix(BLOCK)
    channels = grad.shape[1]
    chunks = pieces[:, :CHUNKS].astype(F32).reshape(RANKS, CHUNKS, 2, ROWS, BLOCK)
    for b in range(2):
        rows = slice(b * BLOCK, (b + 1) * BLOCK)
        turned = flip(unit, chunks[:, :, b].reshape(channels, BLOCK).astype(BF16))
        k_out[rows] = (turned * value[rows].astype(F32)).astype(BF16)
        v_out[rows] = (turned * key[rows].astype(F32)).astype(BF16)
    packed = pieces[:, CHUNKS].astype(F32).reshape(RANKS * 16, BLOCK)
    upper = pltpu.roll(packed, 64, 1).reshape(RANKS, 16, BLOCK)
    both = jnp.stack([packed.reshape(RANKS, 16, BLOCK), upper], 1)
    f_out[...] = flip(unit[:f_out.shape[0]], both.reshape(channels, BLOCK).astype(BF16))


def on_device(out_grad, query_rows, key_rows, value_rows, conv_rows, long_filter, block_table):
    forward, back = tables()
    vmem = pl.BlockSpec(memory_space=pltpu.VMEM)
    units = (RANKS, CHUNKS + 1, 16, BLOCK)
    pieces_u = pltpu.VMEM((RANKS, CHUNKS, 16, BLOCK), BF16)
    dma = pltpu.SemaphoreType.DMA
    rows = jax.ShapeDtypeStruct(out_grad.shape, BF16)
    operands = (block_table, out_grad, query_rows, key_rows, value_rows, long_filter, forward, back)
    pieces = pl.pallas_call(
        exchange_kernel,
        name="exchange",
        out_shape=jax.ShapeDtypeStruct(units, BF16),
        in_specs=[pl.BlockSpec(memory_space=pltpu.HBM)] * 8,
        out_specs=vmem,
        scratch_shapes=[
            pltpu.SMEM((SLOTS,), jnp.int32),
            pltpu.SMEM((SLOTS,), jnp.int32),
            pltpu.VMEM(rows.shape, BF16),
            pltpu.VMEM(rows.shape, BF16),
            pltpu.VMEM(rows.shape, BF16),
            pltpu.VMEM(rows.shape, BF16),
            pltpu.VMEM(long_filter.shape, F32),
            pltpu.VMEM(forward.shape, BF16),
            pltpu.VMEM(back.shape, BF16),
            pltpu.VMEM(units, BF16),
            pltpu.VMEM(units, BF16),
            pieces_u,
            pieces_u,
            pltpu.VMEM(units, BF16),
            pltpu.VMEM((CHUNKS, SLOTS, ROWS, 2 * SPAN), F32),
            pltpu.VMEM((CHUNKS, SLOTS + LAG_BLOCKS - 1, ROWS, SPAN), F32),
            pltpu.VMEM((4, CHUNKS, 2, ROWS, SPAN), F32),
            pltpu.VMEM((LAG_BLOCKS, 32, SPAN), F32),
            pltpu.VMEM((CHUNKS, SLOTS, ROWS, SPAN), F32),
            pltpu.VMEM((CHUNKS, LAG_BLOCKS, ROWS, SPAN), F32),
            dma((8,)),
        ]
        + [dma((len(OFFSETS),))] * 8
        + [dma((2,))],
        compiler_params=pltpu.CompilerParams(
            collective_id=0, has_side_effects=True, vmem_limit_bytes=40 * 1024 * 1024
        ),
    )(*(pltpu.with_memory_space_constraint(x, pltpu.HBM) for x in operands))
    return pl.pallas_call(
        finish_kernel,
        name="finish",
        out_shape=(rows, rows, rows, jax.ShapeDtypeStruct(long_filter.shape, F32)),
        in_specs=[vmem] * 5,
        out_specs=[vmem] * 4,
        compiler_params=pltpu.CompilerParams(vmem_limit_bytes=40 * 1024 * 1024),
    )(out_grad, conv_rows, key_rows, value_rows, pieces)


def solution(mesh):
    rows = P("ctx", "tp")
    return jax.shard_map(
        on_device, mesh=mesh, in_specs=(rows,) * 6 + (P(),), out_specs=(rows,) * 4, check_vma=False
    )
```

time: 27.3 us -> 25.5 us (0.934)
  Pallas kernels: 26.4 us -> 24.7 us
    pallas_call x1, Pallas kernels: 25.3 us -> 23.6 us  [on_device(): pl.pallas_call(exchange_kernel, name='exchange', out_shape=jax.ShapeDtype...]
where the time goes in v3:
time: 25.5 us; the launch traced here: 25.4 us
  Pallas kernels  24.7 us (97%)
  between operations  0.7 us (3%)
    pallas_call x1, Pallas kernels, on_device(): pl.pallas_call(exchange_kernel, name='exchange', out_shape=jax.ShapeDtype...  23.6 us
    pallas_call x1, Pallas kernels, on_device(): pl.pallas_call(finish_kernel, name='finish', out_shape=(rows, rows, rows,...  1.16 us

profile of v3, /device:TPU:1, one launch (start us, length us, event | category | flops | bytes accessed | tf_op | source)
XLA Modules:
  0.0 25.4 jit_solution(8793339249001673103)
XLA Ops:
  0.6 0.0 copy-start.2
  0.6 0.0 copy-start.1
  0.7 0.0 copy-start
  0.7 0.0 copy-start.3
  0.7 23.6 %exchange.1.pieces = bf16[16,5,16,128]{3,2,1,0:T(8,128)(2,1)S(1)} custom-call(s32[32]{0:T(128)} %table_in.1, bf16[256,512]{1,0:T(8,128)(2,1)} %grad.1, bf16[256,512]{1,0:T(8,128)(2,1)} %query_in.1, bf16[256,512]{1,0:T(8,128)(2,1)} %key.1, bf16[256,512]{1,0:T(8,128)(2,1)} %value.1, f32[48,512]{1,0:T(8,128)} %taps_in.1, ...), custom_call_target="tpu_custom_call" | custom-call | tf_op jit(solution)/shard_map/exchange/pallas_call | solution.py:286
  24.2 0.0 copy-done.2
  24.2 0.0 copy-done.1
  24.3 0.0 copy-done
  24.3 0.0 copy-done.3
  24.3 1.2 %finish.1 = (bf16[256,512]{1,0:T(8,128)(2,1)}, bf16[256,512]{1,0:T(8,128)(2,1)}, bf16[256,512]{1,0:T(8,128)(2,1)}, f32[48,512]{1,0:T(8,128)}) custom-call(bf16[256,512]{1,0:T(8,128)(2,1)S(1)} %copy-done, bf16[256,512]{1,0:T(8,128)(2,1)S(1)} %copy-done.3, bf16[256,512]{1,0:T(8,128)(2,1)S(1)} %copy-done.1, bf16[256,512]{1,0:T(8,128)(2,1)S(1)} %copy-done.2, ...), custom_call_target="tpu_custom_call" | custom-call | tf_op jit(solution)/shard_map/finish/pallas_call | solution.py:321
Async XLA Ops:
  0.6 23.6 %copy-start.2 = (bf16[256,512]{1,0:T(8,128)(2,1)S(1)}, bf16[256,512]{1,0:T(8,128)(2,1)}, u32[]{:S(2)}) copy-start(bf16[256,512]{1,0:T(8,128)(2,1)} %value.1) | copy-start | bytes 786436
  0.6 23.6 %copy-start.1 = (bf16[256,512]{1,0:T(8,128)(2,1)S(1)}, bf16[256,512]{1,0:T(8,128)(2,1)}, u32[]{:S(2)}) copy-start(bf16[256,512]{1,0:T(8,128)(2,1)} %key.1) | copy-start | bytes 786436
  0.7 23.6 %copy-start = (bf16[256,512]{1,0:T(8,128)(2,1)S(1)}, bf16[256,512]{1,0:T(8,128)(2,1)}, u32[]{:S(2)}) copy-start(bf16[256,512]{1,0:T(8,128)(2,1)} %grad.1) | copy-start | bytes 786436
  0.7 23.6 %copy-start.3 = (bf16[256,512]{1,0:T(8,128)(2,1)S(1)}, bf16[256,512]{1,0:T(8,128)(2,1)}, u32[]{:S(2)}) copy-start(bf16[256,512]{1,0:T(8,128)(2,1)} %conv.1) | copy-start | bytes 786436

commit v4 on v3

v4 whole, which is shorter than its diff:
```python
import functools

import jax
import jax.numpy as jnp
import numpy as np
from jax import lax
from jax.experimental import pallas as pl
from jax.experimental.pallas import tpu as pltpu
from jax.sharding import PartitionSpec as P

BLOCK = 128
LAG_BLOCKS = 6
SPAN = 2 * BLOCK
RANKS = 16
SLOTS = 2 * RANKS
MESH = pl.DeviceIdType.MESH
F32 = jnp.float32
BF16 = jnp.bfloat16
NT = (((1,), (1,)), ((), ()))


def tables():
    time = np.arange(SPAN)[:, None]
    bins = np.arange(BLOCK)[None, :] + 0.5
    angles = 2.0 * np.pi * time * bins / SPAN
    forward = np.concatenate([np.cos(angles), -np.sin(angles)], 1)
    back = np.concatenate([np.cos(angles[:BLOCK]).T, -np.sin(angles[:BLOCK]).T], 0) * (2.0 / SPAN)
    return jnp.asarray(forward, BF16), jnp.asarray(back, BF16)


def dot(left, right):
    return jnp.dot(left, right, preferred_element_type=F32)


def flip(eye, rows):
    return lax.dot_general(eye, rows, NT, preferred_element_type=F32)


def peer(me, offset):
    dx, dy, dc = offset
    x = lax.rem(lax.div(me, 4) + dx, 4)
    y = lax.rem(lax.rem(lax.div(me, 2), 2) + dy, 2)
    c = lax.rem(lax.rem(me, 2) + dc, 2)
    return (x * 2 + y) * 2 + c


OFFSETS = (
    (2, 1, 1), (2, 1, 0), (1, 1, 1), (3, 1, 0), (3, 1, 1), (1, 1, 0), (2, 0, 1), (0, 1, 0),
    (0, 1, 1), (2, 0, 0), (1, 0, 1), (3, 0, 0), (3, 0, 1), (1, 0, 0), (0, 0, 1),
)


CHUNKS = 4
ROWS = 8
BATCHES = (4, 4, 4, 2, 2)
THIRDS = tuple(slice(i * BLOCK, (i + 1) * BLOCK) for i in range(3))


def load_all(pairs, sems):
    loads = []
    for i, (source, target) in enumerate(pairs):
        load = pltpu.make_async_copy(source, target, sems.at[i])
        load.start()
        loads.append(load)
    return loads


def unit_matrix(size):
    row = lax.broadcasted_iota(jnp.int32, (size, size), 0)
    column = lax.broadcasted_iota(jnp.int32, (size, size), 1)
    return jnp.where(row == column, 1.0, 0.0).astype(BF16)


def exchange_kernel(
    table_in, grad_in, query_in, key_in, value_in, conv_in, taps_in, forward_in, back_in, out, q_out,
    table, inverse, grad, query, key, value, conv, taps, forward, back,
    send_t, recv_t, send_w, recv_w, send_u, recv_u, send_b, spec_h, spec_u,
    spec_w0, spec_w1, spec_w2, spec_w3, spec_v0, spec_v1, spec_v2, spec_v3,
    spec_d0, spec_d1, spec_d2, spec_d3, spec_f0, spec_f1, spec_f2, spec_f3,
    load_sems, t_send, t_recv, w_send, w_recv, u_send, u_recv, d_send, d_recv, f_send, f_recv, own_sems,
):
    spec_w = (spec_w0, spec_w1, spec_w2, spec_w3)
    spec_v = (spec_v0, spec_v1, spec_v2, spec_v3)
    spec_d = (spec_d0, spec_d1, spec_d2, spec_d3)
    spec_f = (spec_f0, spec_f1, spec_f2, spec_f3)
    me = lax.axis_index("ctx")
    peers = [peer(me, offset) for offset in OFFSETS]
    barrier = pltpu.get_barrier_semaphore()
    for to in peers:
        pl.semaphore_signal(barrier, inc=1, device_id={"ctx": to}, device_id_type=MESH)
    sources = [me] + [peer(me, ((4 - dx) % 4, dy, dc)) for dx, dy, dc in OFFSETS]
    loads = load_all(
        ((taps_in, taps), (grad_in, grad), (query_in, query), (key_in, key), (value_in, value),
         (forward_in, forward), (back_in, back), (table_in, table), (conv_in, conv)),
        load_sems,
    )

    def send(source, target, send_sems, recv_sems):
        copies = []
        for i, to in enumerate(peers):
            copy = pltpu.make_async_remote_copy(
                source(to), target, send_sems.at[i], recv_sems.at[i],
                device_id={"ctx": to}, device_id_type=MESH,
            )
            copy.start()
            copies.append(copy)
        return copies

    def keep(source, target, i):
        copy = pltpu.make_async_copy(source, target, own_sems.at[i])
        copy.start()
        return copy

    unit = unit_matrix(SPAN)
    lane = lax.broadcasted_iota(jnp.int32, (16, BLOCK), 1)
    lower = lane < 64
    lags = taps.shape[0]
    loads[0].wait()
    padded = jnp.concatenate([taps[...].astype(BF16), jnp.zeros((BLOCK - lags, taps.shape[1]), BF16)], 0)
    for half in range(2):
        turned = flip(unit, padded[:, half * SPAN:(half + 1) * SPAN])
        for piece in range(8):
            rows = turned[piece * 32:(piece + 1) * 32]
            packed = jnp.where(lower, rows[:16], pltpu.roll(rows[16:], 64, 1))
            send_t[half * 8 + piece] = packed.astype(BF16)

    def cut(left, right, pieces):
        product = (left[...].astype(F32) * right[...].astype(F32)).astype(BF16)
        for half in range(2):
            turned = flip(unit, product[:, half * SPAN:(half + 1) * SPAN]).reshape(8, CHUNKS, ROWS, SPAN)
            for piece in range(8):
                for c in range(CHUNKS):
                    rows = turned[piece, c]
                    pieces[half * 8 + piece, c] = jnp.concatenate(
                        [rows[:, :BLOCK], rows[:, BLOCK:]], 0
                    ).astype(BF16)

    loads[1].wait()
    loads[2].wait()
    cut(grad, query, send_w)
    pl.semaphore_wait(barrier, len(OFFSETS))
    copies_t = send(lambda to: send_t.at[to], recv_t.at[me], t_send, t_recv)
    copies_w = send(lambda to: send_w.at[to], recv_w.at[me], w_send, w_recv)
    own_t = keep(send_t.at[me], recv_t.at[me], 2)
    own_w = keep(send_w.at[me], recv_w.at[me], 0)
    loads[3].wait()
    loads[4].wait()
    cut(key, value, send_u)
    copies_u = send(lambda to: send_u.at[to], recv_u.at[me], u_send, u_recv)
    own_u = keep(send_u.at[me], recv_u.at[me], 1)

    def slot_of(p, carry):
        found = jnp.int32(0)
        for s in range(SLOTS):
            found = jnp.where(table[s] == p, s, found)
        inverse[p] = found
        return carry

    for load in loads[5:]:
        load.wait()
    lax.fori_loop(0, SLOTS, slot_of, 0)
    q_out[...] = (grad[...].astype(F32) * conv[...].astype(F32)).astype(BF16)
    for c in range(CHUNKS):
        spec_v[c][SLOTS:] = jnp.zeros((LAG_BLOCKS - 1, ROWS, 3 * BLOCK), F32)
        spec_f[c][...] = jnp.zeros((LAG_BLOCKS, ROWS, 3 * BLOCK), F32)
    own_t.wait()
    own_w.wait()
    own_u.wait()
    for copy in copies_t:
        copy.wait_recv()

    order = [[jnp.zeros((16, BLOCK), F32) for _ in range(2)] for _ in range(LAG_BLOCKS)]
    for src in range(RANKS):
        first, shift = divmod(src * lags, BLOCK)
        packed = recv_t[src].astype(F32)
        for part in range(2):
            turn = (shift + 64 * part) % BLOCK
            rows = pltpu.roll(packed, turn, 1) if turn else packed
            inside = (lane >= shift) & (lane < shift + lags)
            order[first][part] = jnp.where(inside, rows, order[first][part])
            if shift + lags > BLOCK:
                order[first + 1][part] = jnp.where(lane < shift + lags - BLOCK, rows, order[first + 1][part])
    taps_in_order = jnp.concatenate([part for parts in order for part in parts], 0).astype(BF16)
    spec_h[...] = dot(taps_in_order, forward[:BLOCK]).reshape(LAG_BLOCKS, 32, SPAN)

    for start in range(0, RANKS, 4):
        for copy in copies_w[max(start - 1, 0):start + 3]:
            copy.wait_recv()
        batch = sources[start:start + 4]
        rows_w = jnp.concatenate([recv_w[src].reshape(CHUNKS * 16, BLOCK) for src in batch], 0)
        near = dot(rows_w, forward[:BLOCK]).reshape(4, CHUNKS, 2, ROWS, SPAN)
        later = dot(rows_w, forward[BLOCK:]).reshape(4, CHUNKS, 2, ROWS, SPAN)
        for i, src in enumerate(batch):
            for c in range(CHUNKS):
                spec_w[c][pl.ds(2 * src, 2), :, :SPAN] = near[i, c]
                spec_w[c][pl.ds(2 * src, 2), :, SPAN:] = later[i, c]

    def multiply(c):
        def window(p):
            slot = inverse[p]
            re = spec_w[c][slot, :, :BLOCK]
            im = spec_w[c][slot, :, BLOCK:SPAN]
            if p + 1 < SLOTS:
                after = inverse[p + 1]
                re = re + spec_w[c][after, :, SPAN:SPAN + BLOCK]
                im = im + spec_w[c][after, :, SPAN + BLOCK:]
            spec_v[c][p, :, :BLOCK] = re
            spec_v[c][p, :, BLOCK:SPAN] = im
            both = re + im
            spec_v[c][p, :, SPAN:] = both
            return re, im, both

        group = slice(c * ROWS, (c + 1) * ROWS)
        h = []
        for m in range(LAG_BLOCKS):
            re, im = spec_h[m, group, :BLOCK], spec_h[m, group, BLOCK:]
            h.append((re - im, re + im, re))
        windows = [window(p) for p in range(LAG_BLOCKS - 1)]
        for p in range(SLOTS):
            if p + LAG_BLOCKS - 1 < SLOTS:
                windows.append(window(p + LAG_BLOCKS - 1))
            d = None
            for m in range(min(LAG_BLOCKS, SLOTS - p)):
                v_re, v_im, v_both = windows[p + m]
                term = (h[m][0] * v_im, h[m][1] * v_re, h[m][2] * v_both)
                d = term if d is None else tuple(a + b for a, b in zip(d, term))
            windows[p] = None
            spec_d[c][p, :, :BLOCK] = d[2] - d[0]
            spec_d[c][p, :, BLOCK:] = d[2] - d[1]

    def invert(c):
        rows_d = jnp.concatenate([spec_d[c][table[s]] for s in range(SLOTS)], 0).astype(BF16)
        send_b[:, c] = dot(rows_d, back[...]).astype(BF16).reshape(RANKS, 2 * ROWS, BLOCK)

    copies_d = []
    for c in range(4):
        multiply(c)
        if c:
            invert(c - 1)
    invert(3)
    chunks = pl.ds(0, 4)
    copies_d += send(lambda to: send_b.at[to, chunks], out.at[me, chunks], d_send, d_recv)

    start = 0
    for count in BATCHES:
        for copy in copies_u[max(start - 1, 0):start + count - 1]:
            copy.wait_recv()
        batch = sources[start:start + count]
        start += count
        rows_u = jnp.concatenate([recv_u[src].reshape(CHUNKS * 16, BLOCK) for src in batch], 0)
        spec_u[:count] = dot(rows_u, forward[:BLOCK]).reshape(count, CHUNKS, 2, ROWS, SPAN)
        for c in range(CHUNKS):
            f = [[spec_f[c][m, :, part] for part in THIRDS] for m in range(LAG_BLOCKS)]
            for i, src in enumerate(batch):
                for b in range(2):
                    p = table[2 * src + b]
                    u_re, u_im = spec_u[i, c, b, :, :BLOCK], spec_u[i, c, b, :, BLOCK:]
                    u = (u_re - u_im, u_re + u_im, u_re)
                    for m in range(LAG_BLOCKS):
                        v_re, v_im, v_both = (spec_v[c][p + m, :, part] for part in THIRDS)
                        f[m][0] += u[0] * v_im
                        f[m][1] += u[1] * v_re
                        f[m][2] += u[2] * v_both
            for m in range(LAG_BLOCKS):
                for part, value_f in zip(THIRDS, f[m]):
                    spec_f[c][m, :, part] = value_f
    sums = jnp.concatenate([f[...].reshape(LAG_BLOCKS * ROWS, 3 * BLOCK) for f in spec_f], 0)
    last = sums[:, SPAN:]
    rows_f = jnp.concatenate([last - sums[:, :BLOCK], last - sums[:, BLOCK:SPAN]], 1).astype(BF16)
    scale = float((SLOTS * BLOCK) ** -0.5)
    lagged = (dot(rows_f, back[...]) * scale).reshape(CHUNKS, LAG_BLOCKS, ROWS, BLOCK)
    lag_rows = [
        [jnp.concatenate([lagged[2 * part, m], lagged[2 * part + 1, m]], 0) for part in range(2)]
        for m in range(LAG_BLOCKS)
    ]
    for to in range(RANKS):
        first, shift = divmod(to * lags, BLOCK)
        parts = []
        for part in range(2):
            turn = (64 * part - shift) % BLOCK
            rows = lag_rows[first][part]
            rows = pltpu.roll(rows, turn, 1) if turn else rows
            if shift + lags > BLOCK:
                later = pltpu.roll(lag_rows[first + 1][part], turn, 1)
                rows = jnp.where((lane & 63) < BLOCK - shift, rows, later)
            parts.append(rows)
        send_b[to, CHUNKS] = jnp.where(lower, parts[0], parts[1]).astype(BF16)
    copies_f = send(lambda to: send_b.at[to, CHUNKS], out.at[me, CHUNKS], f_send, f_recv)
    own_b = keep(send_b.at[me], out.at[me], 0)
    for copy in copies_t + copies_w + copies_u:
        copy.wait_send()
    own_b.wait()
    for copy in copies_d + copies_f:
        copy.wait()


def finish_kernel(key, value, pieces, q_in, q_out, k_out, v_out, f_out, k_rows, v_rows, f_rows, sems):
    copies = load_all(((q_in, q_out),), sems)
    unit = unit_matrix(BLOCK)
    channels = key.shape[1]
    packed = pieces[:, CHUNKS].astype(F32).reshape(RANKS * 16, BLOCK)
    upper = pltpu.roll(packed, 64, 1).reshape(RANKS, 16, BLOCK)
    both = jnp.stack([packed.reshape(RANKS, 16, BLOCK), upper], 1)
    f_rows[...] = flip(unit[:f_rows.shape[0]], both.reshape(channels, BLOCK).astype(BF16))
    copies += load_all(((f_rows, f_out),), sems.at[pl.ds(1, 1)])
    chunks = pieces[:, :CHUNKS].astype(F32).reshape(RANKS, CHUNKS, 2, ROWS, BLOCK)
    for b in range(2):
        rows = pl.ds(b * BLOCK, BLOCK)
        turned = flip(unit, chunks[:, :, b].reshape(channels, BLOCK).astype(BF16))
        k_rows[rows] = (turned * value[rows].astype(F32)).astype(BF16)
        v_rows[rows] = (turned * key[rows].astype(F32)).astype(BF16)
        copies += load_all(
            ((k_rows.at[rows], k_out.at[rows]), (v_rows.at[rows], v_out.at[rows])), sems.at[pl.ds(2 + 2 * b, 2)]
        )
    for copy in copies:
        copy.wait()


def on_device(out_grad, query_rows, key_rows, value_rows, conv_rows, long_filter, block_table):
    forward, back = tables()
    vmem = pl.BlockSpec(memory_space=pltpu.VMEM)
    units = (RANKS, CHUNKS + 1, 16, BLOCK)
    pieces_u = pltpu.VMEM((RANKS, CHUNKS, 16, BLOCK), BF16)
    dma = pltpu.SemaphoreType.DMA
    rows = jax.ShapeDtypeStruct(out_grad.shape, BF16)
    operands = (block_table, out_grad, query_rows, key_rows, value_rows, conv_rows, long_filter, forward, back)
    pieces, q_rows = pl.pallas_call(
        exchange_kernel,
        name="exchange",
        out_shape=(jax.ShapeDtypeStruct(units, BF16), rows),
        in_specs=[pl.BlockSpec(memory_space=pltpu.HBM)] * 9,
        out_specs=[vmem] * 2,
        scratch_shapes=[
            pltpu.SMEM((SLOTS,), jnp.int32),
            pltpu.SMEM((SLOTS,), jnp.int32),
            pltpu.VMEM(rows.shape, BF16),
            pltpu.VMEM(rows.shape, BF16),
            pltpu.VMEM(rows.shape, BF16),
            pltpu.VMEM(rows.shape, BF16),
            pltpu.VMEM(rows.shape, BF16),
            pltpu.VMEM(long_filter.shape, F32),
            pltpu.VMEM(forward.shape, BF16),
            pltpu.VMEM(back.shape, BF16),
            pltpu.VMEM((RANKS, 16, BLOCK), BF16),
            pltpu.VMEM((RANKS, 16, BLOCK), BF16),
            pieces_u,
            pieces_u,
            pieces_u,
            pieces_u,
            pltpu.VMEM(units, BF16),
            pltpu.VMEM((LAG_BLOCKS, 32, SPAN), F32),
            pltpu.VMEM((4, CHUNKS, 2, ROWS, SPAN), F32),
        ]
        + [pltpu.VMEM((SLOTS, ROWS, 2 * SPAN), F32)] * CHUNKS
        + [pltpu.VMEM((SLOTS + LAG_BLOCKS - 1, ROWS, 3 * BLOCK), F32)] * CHUNKS
        + [pltpu.VMEM((SLOTS, ROWS, SPAN), F32)] * CHUNKS
        + [pltpu.VMEM((LAG_BLOCKS, ROWS, 3 * BLOCK), F32)] * CHUNKS
        + [dma((9,))]
        + [dma((len(OFFSETS),))] * 10
        + [dma((3,))],
        compiler_params=pltpu.CompilerParams(
            collective_id=0, has_side_effects=True, vmem_limit_bytes=40 * 1024 * 1024
        ),
    )(*(pltpu.with_memory_space_constraint(x, pltpu.HBM) for x in operands))
    return pl.pallas_call(
        finish_kernel,
        name="finish",
        out_shape=(rows, rows, rows, jax.ShapeDtypeStruct(long_filter.shape, F32)),
        in_specs=[vmem] * 4,
        out_specs=[pl.BlockSpec(memory_space=pltpu.HBM)] * 4,
        scratch_shapes=[
            pltpu.VMEM(rows.shape, BF16), pltpu.VMEM(rows.shape, BF16), pltpu.VMEM(long_filter.shape, F32), dma((6,)),
        ],
        compiler_params=pltpu.CompilerParams(vmem_limit_bytes=40 * 1024 * 1024),
    )(key_rows, value_rows, pieces, q_rows)


def solution(mesh):
    rows = P("ctx", "tp")
    return jax.shard_map(
        on_device, mesh=mesh, in_specs=(rows,) * 6 + (P(),), out_specs=(rows,) * 4, check_vma=False
    )
```

time: 25.5 us -> 25.1 us (0.984)
  Pallas kernels: 24.7 us -> 24.3 us
    pallas_call x1, Pallas kernels: 23.6 us -> 23.2 us  [on_device(): pl.pallas_call(exchange_kernel, name='exchange', out_shape=(jax.ShapeDtyp...]
where the time goes in v4:
time: 25.1 us; the launch traced here: 25 us
  Pallas kernels  24.3 us (97%)
  between operations  0.67 us (3%)
    pallas_call x1, Pallas kernels, on_device(): pl.pallas_call(exchange_kernel, name='exchange', out_shape=(jax.ShapeDtyp...  23.2 us
    pallas_call x1, Pallas kernels, on_device(): pl.pallas_call(finish_kernel, name='finish', out_shape=(rows, rows, rows,...  1.15 us

profile of v4, /device:TPU:1, one launch (start us, length us, event | category | flops | bytes accessed | tf_op | source)
XLA Modules:
  0.0 25.0 jit_solution(8691745498004500431)
XLA Ops:
  0.6 0.0 copy-start.1
  0.6 0.0 copy-start
  0.7 23.2 %exchange.1 = (bf16[16,5,16,128]{3,2,1,0:T(8,128)(2,1)S(1)}, bf16[256,512]{1,0:T(8,128)(2,1)S(1)}) custom-call(s32[32]{0:T(128)} %table_in.1, bf16[256,512]{1,0:T(8,128)(2,1)} %grad_in.1, bf16[256,512]{1,0:T(8,128)(2,1)} %query_in.1, bf16[256,512]{1,0:T(8,128)(2,1)} %key.1, bf16[256,512]{1,0:T(8,128)(2,1)} %value.1, bf16[256,512]{1,0:T(8,128)(2,1)} %conv_in.1, ...), custom_call_target="tpu_custom_call" | custom-call | tf_op jit(solution)/shard_map/exchange/pallas_call | solution.py:327
  23.9 0.0 copy-done.1
  23.9 0.0 copy-done
  23.9 1.2 %finish.1 = (bf16[256,512]{1,0:T(8,128)(2,1)}, bf16[256,512]{1,0:T(8,128)(2,1)}, bf16[256,512]{1,0:T(8,128)(2,1)}, f32[48,512]{1,0:T(8,128)}) custom-call(bf16[256,512]{1,0:T(8,128)(2,1)S(1)} %copy-done, bf16[256,512]{1,0:T(8,128)(2,1)S(1)} %copy-done.1, bf16[16,5,16,128]{3,2,1,0:T(8,128)(2,1)S(1)} %get-tuple-element.6.pieces, ...), custom_call_target="tpu_custom_call" | custom-call | tf_op jit(solution)/shard_map/finish/pallas_call | solution.py:365
Async XLA Ops:
  0.6 23.2 %copy-start.1 = (bf16[256,512]{1,0:T(8,128)(2,1)S(1)}, bf16[256,512]{1,0:T(8,128)(2,1)}, u32[]{:S(2)}) copy-start(bf16[256,512]{1,0:T(8,128)(2,1)} %value.1) | copy-start | bytes 786436
  0.6 23.2 %copy-start = (bf16[256,512]{1,0:T(8,128)(2,1)S(1)}, bf16[256,512]{1,0:T(8,128)(2,1)}, u32[]{:S(2)}) copy-start(bf16[256,512]{1,0:T(8,128)(2,1)} %key.1) | copy-start | bytes 786436

commit v5 on v4

--- a/solution.py
+++ b/solution.py
@@ -52,7 +52,7 @@
 
 CHUNKS = 4
 ROWS = 8
-BATCHES = (4, 4, 4, 2, 2)
+BATCHES = (4, 4, 4, 3, 1)
 THIRDS = tuple(slice(i * BLOCK, (i + 1) * BLOCK) for i in range(3))
 
 
@@ -287,11 +287,11 @@
         send_b[to, CHUNKS] = jnp.where(lower, parts[0], parts[1]).astype(BF16)
     copies_f = send(lambda to: send_b.at[to, CHUNKS], out.at[me, CHUNKS], f_send, f_recv)
     own_b = keep(send_b.at[me], out.at[me], 0)
-    for copy in copies_t + copies_w + copies_u:
+    own_b.wait()
+    for copy in copies_t + copies_w + copies_u + copies_d + copies_f:
         copy.wait_send()
-    own_b.wait()
-    for copy in copies_d + copies_f:
-        copy.wait()
+    for copy in copies_d + copies_f[::-1]:
+        copy.wait_recv()
 
 
 def finish_kernel(key, value, pieces, q_in, q_out, k_out, v_out, f_out, k_rows, v_rows, f_rows, sems):

time: 25.1 us -> 25.1 us (level)
  no operation moved by 1% of the time
where the time goes in v5:
time: 25.1 us; the launch traced here: 25 us
  Pallas kernels  24.3 us (97%)
  between operations  0.67 us (3%)
    pallas_call x1, Pallas kernels, on_device(): pl.pallas_call(exchange_kernel, name='exchange', out_shape=(jax.ShapeDtyp...  23.1 us
    pallas_call x1, Pallas kernels, on_device(): pl.pallas_call(finish_kernel, name='finish', out_shape=(rows, rows, rows,...  1.15 us

profile of v5, /device:TPU:1, one launch (start us, length us, event | category | flops | bytes accessed | tf_op | source)
XLA Modules:
  0.0 25.0 jit_solution(4285441947934642202)
XLA Ops:
  0.6 0.0 copy-start.1
  0.6 0.0 copy-start
  0.7 23.1 %exchange.1 = (bf16[16,5,16,128]{3,2,1,0:T(8,128)(2,1)S(1)}, bf16[256,512]{1,0:T(8,128)(2,1)S(1)}) custom-call(s32[32]{0:T(128)} %table_in.1, bf16[256,512]{1,0:T(8,128)(2,1)} %grad_in.1, bf16[256,512]{1,0:T(8,128)(2,1)} %query_in.1, bf16[256,512]{1,0:T(8,128)(2,1)} %key.1, bf16[256,512]{1,0:T(8,128)(2,1)} %value.1, bf16[256,512]{1,0:T(8,128)(2,1)} %conv_in.1, ...), custom_call_target="tpu_custom_call" | custom-call | tf_op jit(solution)/shard_map/exchange/pallas_call | solution.py:327
  23.8 0.0 copy-done.1
  23.8 0.0 copy-done
  23.8 1.2 %finish.1 = (bf16[256,512]{1,0:T(8,128)(2,1)}, bf16[256,512]{1,0:T(8,128)(2,1)}, bf16[256,512]{1,0:T(8,128)(2,1)}, f32[48,512]{1,0:T(8,128)}) custom-call(bf16[256,512]{1,0:T(8,128)(2,1)S(1)} %copy-done, bf16[256,512]{1,0:T(8,128)(2,1)S(1)} %copy-done.1, bf16[16,5,16,128]{3,2,1,0:T(8,128)(2,1)S(1)} %get-tuple-element.6.pieces, ...), custom_call_target="tpu_custom_call" | custom-call | tf_op jit(solution)/shard_map/finish/pallas_call | solution.py:365
Async XLA Ops:
  0.6 23.2 %copy-start.1 = (bf16[256,512]{1,0:T(8,128)(2,1)S(1)}, bf16[256,512]{1,0:T(8,128)(2,1)}, u32[]{:S(2)}) copy-start(bf16[256,512]{1,0:T(8,128)(2,1)} %value.1) | copy-start | bytes 786436
  0.6 23.2 %copy-start = (bf16[256,512]{1,0:T(8,128)(2,1)S(1)}, bf16[256,512]{1,0:T(8,128)(2,1)}, u32[]{:S(2)}) copy-start(bf16[256,512]{1,0:T(8,128)(2,1)} %key.1) | copy-start | bytes 786436
